TPU v7x, 32 devices: a whole 2x2x4 slice. The times are simulated.
32 devices in a mesh: orb: 8 (over z, x), wall: 4 (over y, core).
Axes of the slice: x: 2, y: 2, z: 4, core: 2. Of those that a mesh axis runs over, the one named last changes fastest.
Arguments:
- fluid_state: float32 [8, 98304], P(None, ('orb', 'wall')), may hold values from -4 to 4, as said below
- ghost_list: int32 [7, 192], P(None, ('orb', 'wall')), may hold values from 0 to 23, as said below
- pair_list: int32 [768, 14], P(('orb', 'wall')), may hold values from 0 to 65, as said below
- wall_state: float32 [4, 24576], P(None, ('orb', 'wall')), may hold values from 0 to 0.6, as said below
- wall_count: int32 [192], P(('orb', 'wall')), may hold values from 1 to 128, as said below
- wall_pairs: int32 [768, 4], P(('orb', 'wall')), may hold values from 0 to 7, as said below
Outputs:
- density_rate: float32 [98304], P(('orb', 'wall'))
- acceleration: float32 [3, 98304], P(None, ('orb', 'wall'))
- time_step: float32 [], replicated
Inputs may be any that keep to these rules, and one draw needn't show every extreme that they name: `fluid_state`: rows: position from 0 to 0.6, velocity from -4 to 4, density from 0.97 to 1.03, mass from 0.001 to 0.003. `ghost_list`: the 6 entries of one mask and one domain are distinct. `pair_list`: the 14 entries of one block are distinct, and every candidate index is named by some block of each domain. `wall_state`: rows: x and y from 0 to 0.6, z from 0 to 0.15, mass from 0.001 to 0.003. `wall_count`: the live particles fill the first columns of their wall block. `wall_pairs`: the 4 entries of one block are distinct, and every wall candidate index is named by some block of each domain.
All inputs are finite; a program needn't handle non-finite values.
Results may differ from a plain program's by a relative error of at most 0.0003.
Values sent between devices are 32-bit elements; how exact they have to be, the bound alone decides.
No kernel may reach another device: no remote copies, remote signals or barrier semaphores. Data moves between devices by JAX's collectives and lax.ppermute only.
A program may use at most 64 MiB of HBM per device.

v0:
```python
import functools

import jax
import jax.numpy as jnp
from jax import lax
from jax.experimental import pallas as pl
from jax.experimental.pallas import tpu as pltpu
from jax.sharding import PartitionSpec as P

EB = 1
LANES = 128
FEATURES = 64
MOMENTS = 16

smoothing = 0.1
support = 0.3
kernel_norm = 21.0 / (2.0 * 3.141592653589793 * support**3)
grad_coeff = -20.0 / support**2 * kernel_norm
tait_coeff = 25.0 / 7.0
visc_coeff = 0.05
cohesion = 2000.0
adhesion = 2000.0
gravity = 9.81
courant = 0.25

center = 0.3
shift = 0.0001 / support**2
approach_coeff = grad_coeff * visc_coeff * 2.0 / (support * 4.0 * cohesion)

SPLITS = ((0, 0), (0, 1), (1, 0), (0, 2), (2, 0), (1, 1), (1, 2), (2, 1))


def rounded(value):
    return value.astype(jnp.bfloat16).astype(jnp.float32)


def split(value):
    first = rounded(value)
    rest = value - first
    second = rounded(rest)
    return (first, second, rest - second)


def dotted(left, right):
    return left[0] * right[0] + left[1] * right[1] + left[2] * right[2]


def pressure_ratio(density):
    square = density * density
    return tait_coeff * (square * square * square * density - 1.0) / square


def loaded(ref, row, count, stride):
    return ref[pl.ds(row, count, stride=stride), :]


def scaled_position(ref, count, stride):
    return [(loaded(ref, d, count, stride) - center) * (1.0 / support) for d in range(3)]


def source_rows(pos, vel, density):
    one = jnp.ones_like(pos[0])
    rows = [one, one, one]
    rows += split(dotted(pos, pos))
    if vel is not None:
        rows += split(approach_coeff * dotted(pos, vel))
    else:
        rows += [one * 0.0] * 3
    for d in range(3):
        pieces = split(pos[d])
        rows += [pieces[t] for _, t in SPLITS]
    if vel is not None:
        for d in range(3):
            pieces = split(vel[d])
            rows += [pieces[t] for _, t in SPLITS]
    zero = one * 0.0
    rows += [zero] * (FEATURES - len(rows))
    if density is not None:
        rows[FEATURES - 1] = density
    return rows


def target_rows(pos, vel):
    one = jnp.ones_like(pos[0])
    zero = one * 0.0
    near = list(split(dotted(pos, pos))) + [one] * 3 + [zero] * 3
    along = list(split(approach_coeff * dotted(pos, vel))) + [zero] * 3 + [one] * 3
    for d in range(3):
        pieces = split(-2.0 * pos[d])
        near += [pieces[p] for p, _ in SPLITS]
        pieces = split(-approach_coeff * vel[d])
        along += [pieces[p] for p, _ in SPLITS]
    for d in range(3):
        pieces = split(-approach_coeff * pos[d])
        along += [pieces[p] for p, _ in SPLITS]
    near += [zero] * (FEATURES - len(near))
    along += [zero] * (FEATURES - len(along))
    return near, along


def moment_rows(pos, vel, mass, own, other):
    columns = [other] + [other * p for p in pos]
    columns += [own] + [own * p for p in pos]
    columns += [mass] + [mass * p for p in pos]
    if vel is not None:
        columns += [mass * v for v in vel] + [mass * dotted(pos, vel)]
    else:
        columns += [mass * 0.0] * 4
    pieces = [split(column) for column in columns]
    return [pieces[c][p] for p in range(3) for c in range(MOMENTS)]


def put_sources(rows, moments, count, base, stage, src, mom, rho):
    for k, row in enumerate(rows):
        stage[pl.ds(k, count, stride=FEATURES), :] = row

    def turn(b, carry):
        block = stage[pl.ds(pl.multiple_of(b * FEATURES, FEATURES), FEATURES), :]
        turned = block.T
        src[base + b] = turned.astype(jnp.bfloat16)
        if rho is not None:
            rho[base + b] = jnp.broadcast_to(turned[:, FEATURES - 1 :], (LANES, LANES))
        return carry

    lax.fori_loop(0, count, turn, 0)
    depth = 3 * MOMENTS
    for k, row in enumerate(moments):
        stage[pl.ds(k, count, stride=depth), :] = row

    def place(b, carry):
        block = stage[pl.ds(pl.multiple_of(b * depth, depth), depth), :].astype(jnp.bfloat16)
        mom[base + b] = jnp.concatenate([block, block], axis=1)
        return carry

    lax.fori_loop(0, count, place, 0)


def fluid_sources(ref, count, base, stage, src, mom, rho):
    pos = scaled_position(ref, count, 8)
    vel = [loaded(ref, 3 + d, count, 8) for d in range(3)]
    density = loaded(ref, 6, count, 8)
    mass = loaded(ref, 7, count, 8)
    other = mass * (3.0 * cohesion + grad_coeff * pressure_ratio(density))
    rows = source_rows(pos, vel, density)
    put_sources(rows, moment_rows(pos, vel, mass, mass, other), count, base, stage, src, mom, rho)


def wall_sources(ref, count, stage, src, mom):
    pos = scaled_position(ref, count, 4)
    mass = loaded(ref, 3, count, 4)
    rows = source_rows(pos, None, None)
    moments = moment_rows(pos, None, mass, 2.0 * mass, (3.0 * adhesion) * mass)
    put_sources(rows, moments, count, 0, stage, src, mom, None)


def put_targets(ref, count, stage, tgt):
    pos = scaled_position(ref, count, 8)
    vel = [loaded(ref, 3 + d, count, 8) for d in range(3)]
    for half, rows in enumerate(target_rows(pos, vel)):
        for k, row in enumerate(rows):
            stage[pl.ds(k, count, stride=FEATURES), :] = row

        def place(b, carry):
            block = stage[pl.ds(pl.multiple_of(b * FEATURES, FEATURES), FEATURES), :]
            tgt[b, :, half * LANES : (half + 1) * LANES] = block.astype(jnp.bfloat16)
            return carry

        lax.fori_loop(0, count, place, 0)


def in_two(value):
    high = value.astype(jnp.bfloat16)
    return high, (value - high.astype(jnp.float32)).astype(jnp.bfloat16)


def falloff_of(dist_sq):
    guarded = jnp.maximum(dist_sq, 1e-30)
    root = guarded * lax.rsqrt(guarded)
    falloff = jnp.maximum(1.0 - root, 0.0)
    return guarded, falloff, falloff * falloff * falloff


def weighted(moments, cubed, blend):
    cubed_high, cubed_low = in_two(cubed)
    blend_high, blend_low = in_two(blend)
    weights = jnp.concatenate(
        [
            jnp.concatenate([cubed_high, blend_high], axis=1),
            jnp.concatenate([cubed_low, blend_low], axis=1),
        ],
        axis=0,
    )
    return jnp.dot(moments, weights, preferred_element_type=jnp.float32)


def pair_kernel(
    blocks, walls, own_ref, ghost_ref, wall_ref, pair_ref, wpair_ref, place_ref,
    rate_ref, accel_ref, peak_ref, stage, src, mom, rho, wsrc, wmom, tgt,
    acc_cubed, acc_blend, table,
):
    ghosts = ghost_ref.shape[0] // 8
    per_mask = ghosts // 8
    place = place_ref[0]
    for c in range(blocks):
        table[c] = c
    for mask in range(1, 8):
        for g in range(per_mask):
            table[blocks + (mask - 1) * per_mask + g] = (
                blocks + jnp.bitwise_xor(place, mask) * per_mask + g
            )
    fluid_sources(own_ref, blocks, 0, stage, src, mom, rho)
    fluid_sources(ghost_ref, ghosts, blocks, stage, src, mom, rho)
    wall_sources(wall_ref, walls, stage, wsrc, wmom)
    put_targets(own_ref, blocks, stage, tgt)

    def per_target(b, carry):
        target = tgt[b]
        target_rho = own_ref[pl.ds(b * 8 + 6, 1), :]
        total = jnp.zeros((3 * MOMENTS, 2 * LANES), jnp.float32)
        for k in range(pair_ref.shape[1]):
            s = table[pair_ref[b, k]]
            product = jnp.dot(src[s], target, preferred_element_type=jnp.float32)
            guarded, falloff, cubed = falloff_of(product[:, :LANES])
            approach = product[:, LANES:]
            spread = (guarded + shift) * (rho[s] + target_rho)
            viscous = jnp.maximum(approach, 0.0) / spread
            total += weighted(mom[s], cubed, cubed * (falloff + viscous))
        for k in range(wpair_ref.shape[1]):
            s = wpair_ref[b, k]
            product = jnp.dot(wsrc[s], target[:, :LANES], preferred_element_type=jnp.float32)
            _, falloff, cubed = falloff_of(product)
            total += weighted(wmom[s], cubed, cubed * falloff)
        folded = total[:MOMENTS] + total[MOMENTS : 2 * MOMENTS] + total[2 * MOMENTS :]
        rows = pl.ds(pl.multiple_of(b * MOMENTS, MOMENTS), MOMENTS)
        acc_cubed[rows, :] = folded[:, :LANES]
        acc_blend[rows, :] = folded[:, LANES:]
        return carry

    lax.fori_loop(0, blocks, per_target, 0)

    pos = scaled_position(own_ref, blocks, 8)
    vel = [loaded(own_ref, 3 + d, blocks, 8) for d in range(3)]
    own_press = grad_coeff * pressure_ratio(loaded(own_ref, 6, blocks, 8))

    def summed(row, ref=acc_cubed):
        return loaded(ref, row, blocks, MOMENTS)

    mass_sum = summed(8)
    mass_pos = [summed(9 + d) for d in range(3)]
    mass_vel = [summed(12 + d) for d in range(3)]
    rate = dotted(pos, vel) * mass_sum - dotted(vel, mass_pos) - dotted(pos, mass_vel) + summed(15)
    rate_ref[...] = (support * grad_coeff) * rate
    square = jnp.zeros_like(rate)
    for d in range(3):
        force = pos[d] * summed(0) - summed(1 + d)
        force += own_press * (pos[d] * summed(4) - summed(5 + d))
        force -= (4.0 * cohesion) * (pos[d] * summed(8, acc_blend) - summed(9 + d, acc_blend))
        force = -support * force
        if d == 2:
            force -= gravity
        square += force * force
        stage[pl.ds(d, blocks, stride=8), :] = force
    for b in range(blocks):
        accel_ref[:, b * LANES : (b + 1) * LANES] = stage[b * 8 : b * 8 + 3, :]
    peak_ref[...] = jnp.full(peak_ref.shape, jnp.sqrt(jnp.max(square)), jnp.float32)


def pair_pass(own, ghosts, walls, pair_list, wall_pairs, place):
    blocks = own.shape[0] // 8
    ghost_blocks = ghosts.shape[0] // 8
    wall_blocks = walls.shape[0] // 4
    total = blocks + ghost_blocks
    depth = 3 * MOMENTS
    smem = pl.BlockSpec(memory_space=pltpu.SMEM)
    vmem = pl.BlockSpec(memory_space=pltpu.VMEM)
    return pl.pallas_call(
        functools.partial(pair_kernel, blocks, wall_blocks),
        out_shape=(
            jax.ShapeDtypeStruct((blocks, LANES), jnp.float32),
            jax.ShapeDtypeStruct((3, blocks * LANES), jnp.float32),
            jax.ShapeDtypeStruct((8, LANES), jnp.float32),
        ),
        in_specs=[vmem, vmem, vmem, smem, smem, smem],
        out_specs=(vmem, vmem, vmem),
        scratch_shapes=[
            pltpu.VMEM((ghost_blocks * FEATURES, LANES), jnp.float32),
            pltpu.VMEM((total, LANES, FEATURES), jnp.bfloat16),
            pltpu.VMEM((total, depth, 2 * LANES), jnp.bfloat16),
            pltpu.VMEM((total, LANES, LANES), jnp.float32),
            pltpu.VMEM((wall_blocks, LANES, FEATURES), jnp.bfloat16),
            pltpu.VMEM((wall_blocks, depth, 2 * LANES), jnp.bfloat16),
            pltpu.VMEM((blocks, FEATURES, 2 * LANES), jnp.bfloat16),
            pltpu.VMEM((blocks * MOMENTS, LANES), jnp.float32),
            pltpu.VMEM((blocks * MOMENTS, LANES), jnp.float32),
            pltpu.SMEM((total,), jnp.int32),
        ],
        compiler_params=pltpu.CompilerParams(vmem_limit_bytes=40 * 1024 * 1024),
        name="pair_pass",
    )(own, ghosts, walls, pair_list, wall_pairs, place)


def swapped(shard, axis, bit):
    return lax.ppermute(shard, axis, [(i, i ^ 1 << bit) for i in range(lax.axis_size(axis))])


def padded(block, sides, width):
    for axis, dim in sides:
        count = lax.axis_size(axis)
        forward = [(i, i + 1) for i in range(count - 1)]
        backward = [(target, source) for source, target in forward]
        low = lax.ppermute(
            lax.slice_in_dim(block, block.shape[dim] - width, None, axis=dim), axis, forward
        )
        high = lax.ppermute(lax.slice_in_dim(block, 0, width, axis=dim), axis, backward)
        block = jnp.concatenate([low, block, high], axis=dim)
    return block


def per_device(fluid_state, ghost_list, pair_list, wall_state, wall_count, wall_pairs):
    block_total = fluid_state.shape[1] // LANES
    own_blocks = jnp.transpose(fluid_state.reshape(8, block_total, LANES), (1, 0, 2))
    place = lax.axis_index("orb") % 8
    slots = jnp.bitwise_xor(jnp.arange(8, dtype=jnp.int32), place)
    own_slot = jnp.zeros((1, ghost_list.shape[1]), jnp.int32)
    sent = own_blocks[jnp.concatenate([own_slot, ghost_list], axis=0)[slots]]
    groups = [list(range(g, g + 8)) for g in range(0, lax.axis_size("orb"), 8)]
    landed = lax.all_to_all(
        sent, "orb", 0, 0, axis_index_groups=groups if len(groups) > 1 else None
    )
    alive = (
        (jnp.arange(LANES, dtype=jnp.int32)[None, :] < wall_count[:, None])
        .astype(jnp.float32)
        .reshape(-1)
    )
    wall_live = jnp.concatenate([wall_state[0:3], wall_state[3:4] * alive[None, :]], axis=0)
    extended = padded(wall_live, (("wall", 1),), EB * LANES)
    wall_cands = jnp.transpose(extended.reshape(4, -1, LANES), (1, 0, 2))
    rate, acceleration, local_peak = pair_pass(
        own_blocks.reshape(-1, LANES),
        landed.reshape(-1, LANES),
        wall_cands.reshape(-1, LANES),
        pair_list,
        wall_pairs,
        place.reshape(1),
    )
    peak = local_peak[0, 0]
    for axis in ("wall", "orb"):
        for bit in range((lax.axis_size(axis) - 1).bit_length()):
            peak = jnp.maximum(peak, swapped(peak, axis, bit))
    time_step = courant * jnp.sqrt(smoothing / (peak + 1e-06))
    return (rate.reshape(-1), acceleration, time_step)


def solution(mesh):
    return jax.shard_map(
        per_device,
        mesh=mesh,
        in_specs=(
            P(None, ("orb", "wall")),
            P(None, ("orb", "wall")),
            P(("orb", "wall"), None),
            P(None, ("orb", "wall")),
            P(("orb", "wall")),
            P(("orb", "wall"), None),
        ),
        out_specs=(P(("orb", "wall")), P(None, ("orb", "wall")), P()),
        check_vma=False,
    )
```

profile of v0, /device:TPU:0, one launch (start us, length us, event | category | flops | bytes accessed | tf_op | source)
XLA Modules:
  0.0 89.5 jit_solution(2495366264758389012)
XLA Ops:
  0.7 0.7 concatenate.9
  1.4 0.6 gather_fusion
  1.9 0.1 reshape.96
  2.0 1.3 %gather_fusion.1 = f32[48,8,128]{2,1,0:T(8,128)} fusion(f32[24,8,128]{2,1,0:T(8,128)S(1)} %bitcast.27, s32[1024]{0:T(1024)S(1)} %pad_clamp_fusion), kind=kCustom, calls=%fused_computation.1 | custom fusion | bytes 393408 | tf_op jit(solution)/shard_map/gather | solution.py:325
  3.3 7.4 %all-to-all-start = ((f32[8,6,8,128]{3,2,1,0:T(8,128)}), f32[8,6,8,128]{3,2,1,0:T(8,128)S(1)}, u32[]{:S(2)}, u32[]{:S(2)}) async-start(f32[8,6,8,128]{3,2,1,0:T(8,128)} %bitcast.6), calls=%async_computation | async-start | bytes 393216 | tf_op jit(solution)/shard_map/all_to_all | solution.py:327
  10.7 0.1 fusion
  10.8 1.5 %collective-permute-start = (f32[4,128]{1,0:T(4,128)S(1)}, f32[4,128]{1,0:T(4,128)S(1)}, u32[]{:S(2)}, u32[]{:S(2)}) collective-permute-start(f32[4,128]{1,0:T(4,128)S(1)} %get-tuple-element.9), channel_id=1, source_target_pairs={{0,1},{1,2},{2,3},{4,5},{5,6},{6,7},{8,9},{9,10},{10,11},{12,13},{... | collective-permute-start | bytes 6152 | tf_op jit(solution)/shard_map/ppermute | solution.py:311
  12.3 1.3 %collective-permute-start.1 = (f32[4,128]{1,0:T(4,128)S(1)}, f32[4,128]{1,0:T(4,128)S(1)}, u32[]{:S(2)}, u32[]{:S(2)}) collective-permute-start(f32[4,128]{1,0:T(4,128)S(1)} %get-tuple-element.10), channel_id=1, source_target_pairs={{1,0},{2,1},{3,2},{5,4},{6,5},{7,6},{9,8},{10,9},{11,10},{13,12},{... | collective-permute-start | bytes 6152 | tf_op jit(solution)/shard_map/ppermute | solution.py:314
  13.6 0.1 copy.13.pair_ref
  13.7 0.1 copy.14.wpair_ref
  13.8 3.2 %collective-permute-done.1 = f32[4,128]{1,0:T(4,128)S(1)} collective-permute-done((f32[4,128]{1,0:T(4,128)S(1)}, f32[4,128]{1,0:T(4,128)S(1)}, u32[]{:S(2)}, u32[]{:S(2)}) %collective-permute-start.1) | collective-permute-done | bytes 2080 | tf_op jit(solution)/shard_map/ppermute | solution.py:314
  17.0 1.7 %all-to-all-done = f32[8,6,8,128]{3,2,1,0:T(8,128)S(1)} async-done(((f32[8,6,8,128]{3,2,1,0:T(8,128)}), f32[8,6,8,128]{3,2,1,0:T(8,128)S(1)}, u32[]{:S(2)}, u32[]{:S(2)}) %all-to-all-start) | async-done | bytes 196640 | tf_op jit(solution)/shard_map/all_to_all | solution.py:327
  18.7 48.6 %pair_pass.1 = (f32[24,128]{1,0:T(8,128)}, f32[3,3072]{1,0:T(4,128)}, f32[8,128]{1,0:T(8,128)S(1)}) custom-call(f32[192,128]{1,0:T(8,128)S(1)} %bitcast.28, f32[384,128]{1,0:T(8,128)S(1)} %bitcast.29, f32[32,128]{1,0:T(8,128)S(1)} %bitcast.30, s32[24,14]{1,0:T(8,128)S(1)} %copy.13.pair_ref, s32[24,4]{1,0:T(8,128)S(1)} %copy.14.wpair_ref, s32[1]{0:T(128)} %bitcast.11.place_ref), custom_call_target="tpu_custom_call" | custom-call | tf_op jit(solution)/shard_map/pair_pass/pallas_call | solution.py:276
  67.2 0.5 slice.19
  67.7 0.6 collective-permute-start.2
  68.4 1.0 %collective-permute-done.2 = f32[]{:T(128)} collective-permute-done((f32[]{:T(128)}, f32[]{:T(128)}, u32[]{:S(2)}, u32[]{:S(2)}) %collective-permute-start.2) | collective-permute-done | bytes 36 | tf_op jit(solution)/shard_map/ppermute | solution.py:303
  70.6 2.5 %collective-permute-start.3 = (f32[]{:T(128)}, f32[]{:T(128)}, u32[]{:S(2)}, u32[]{:S(2)}) collective-permute-start(f32[]{:T(128)} %max.15), channel_id=1, source_target_pairs={{0,2},{1,3},{2,0},{3,1},{4,6},{5,7},{6,4},{7,5},{8,10},{9,11},{10,... | collective-permute-start | bytes 20 | tf_op jit(solution)/shard_map/ppermute | solution.py:303
  73.1 1.1 %collective-permute-done.3 = f32[]{:T(128)} collective-permute-done((f32[]{:T(128)}, f32[]{:T(128)}, u32[]{:S(2)}, u32[]{:S(2)}) %collective-permute-start.3) | collective-permute-done | bytes 36 | tf_op jit(solution)/shard_map/ppermute | solution.py:303
  74.8 3.4 %collective-permute-start.4 = (f32[]{:T(128)}, f32[]{:T(128)}, u32[]{:S(2)}, u32[]{:S(2)}) collective-permute-start(f32[]{:T(128)} %max.16), channel_id=1, source_target_pairs={{0,4},{4,0},{8,12},{12,8},{16,20},{20,16},{24,28},{28,24},{1,5},{5... | collective-permute-start | bytes 20 | tf_op jit(solution)/shard_map/ppermute | solution.py:303
  78.2 0.2 collective-permute-done.4
  79.0 3.4 %collective-permute-start.5 = (f32[]{:T(128)}, f32[]{:T(128)}, u32[]{:S(2)}, u32[]{:S(2)}) collective-permute-start(f32[]{:T(128)} %max.17), channel_id=1, source_target_pairs={{0,8},{4,12},{8,0},{12,4},{16,24},{20,28},{24,16},{28,20},{1,9},{5... | collective-permute-start | bytes 20 | tf_op jit(solution)/shard_map/ppermute | solution.py:303
  82.4 0.2 collective-permute-done.5
  83.2 4.3 %collective-permute-start.6 = (f32[]{:T(128)}, f32[]{:T(128)}, u32[]{:S(2)}, u32[]{:S(2)}) collective-permute-start(f32[]{:T(128)} %max.18), channel_id=1, source_target_pairs={{0,16},{4,20},{8,24},{12,28},{16,0},{20,4},{24,8},{28,12},{1,17},{... | collective-permute-start | bytes 20 | tf_op jit(solution)/shard_map/ppermute | solution.py:303
  87.5 0.2 collective-permute-done.6
  (18 shorter events, 0.1 us)
Async XLA Ops:
  0.6 1.4 %copy-start = (f32[8,3072]{1,0:T(8,128)S(1)}, f32[8,3072]{1,0:T(8,128)}, u32[]{:S(2)}) copy-start(f32[8,3072]{1,0:T(8,128)} %param.6) | copy-start | bytes 294916
  3.3 7.4 %copy-start.4 = (s32[6]{0:T(128)S(1)}, s32[6]{0:T(128)}, u32[]{:S(2)}) copy-start(s32[6]{0:T(128)} %param.10) | copy-start | bytes 76
  3.3 7.5 %copy-start.1 = (f32[4,768]{1,0:T(4,128)S(1)}, f32[4,768]{1,0:T(4,128)}, u32[]{:S(2)}) copy-start(f32[4,768]{1,0:T(4,128)} %param.9) | copy-start | bytes 36868
  3.3 15.3 %all-to-all-start = ((f32[8,6,8,128]{3,2,1,0:T(8,128)}), f32[8,6,8,128]{3,2,1,0:T(8,128)S(1)}, u32[]{:S(2)}, u32[]{:S(2)}) async-start(f32[8,6,8,128]{3,2,1,0:T(8,128)} %bitcast.6), calls=%async_computation | async-start | bytes 393216 | tf_op jit(solution)/shard_map/all_to_all | solution.py:327
  10.8 2.8 %copy-start.2 = (s32[24,14]{0,1:T(8,128)S(1)}, s32[24,14]{0,1:T(8,128)}, u32[]{:S(2)}) copy-start(s32[24,14]{0,1:T(8,128)} %param.8) | copy-start | bytes 4036
  10.8 3.0 %collective-permute-start = (f32[4,128]{1,0:T(4,128)S(1)}, f32[4,128]{1,0:T(4,128)S(1)}, u32[]{:S(2)}, u32[]{:S(2)}) collective-permute-start(f32[4,128]{1,0:T(4,128)S(1)} %get-tuple-element.9), channel_id=1, source_target_pairs={{0,1},{1,2},{2,3},{4,5},{5,6},{6,7},{8,9},{9,10},{10,11},{12,13},{... | collective-permute-start | bytes 6152 | tf_op jit(solution)/shard_map/ppermute | solution.py:311
  12.3 1.4 %copy-start.3 = (s32[24,4]{0,1:T(4,128)S(1)}, s32[24,4]{0,1:T(4,128)}, u32[]{:S(2)}) copy-start(s32[24,4]{0,1:T(4,128)} %param.11) | copy-start | bytes 1156
  12.3 4.6 %collective-permute-start.1 = (f32[4,128]{1,0:T(4,128)S(1)}, f32[4,128]{1,0:T(4,128)S(1)}, u32[]{:S(2)}, u32[]{:S(2)}) collective-permute-start(f32[4,128]{1,0:T(4,128)S(1)} %get-tuple-element.10), channel_id=1, source_target_pairs={{1,0},{2,1},{3,2},{5,4},{6,5},{7,6},{9,8},{10,9},{11,10},{13,12},{... | collective-permute-start | bytes 6152 | tf_op jit(solution)/shard_map/ppermute | solution.py:314
  67.7 1.6 %collective-permute-start.2 = (f32[]{:T(128)}, f32[]{:T(128)}, u32[]{:S(2)}, u32[]{:S(2)}) collective-permute-start(f32[]{:T(128)} %bitcast.13), channel_id=1, source_target_pairs={{0,1},{1,0},{2,3},{3,2},{4,5},{5,4},{6,7},{7,6},{8,9},{9,8},{10,11... | collective-permute-start | bytes 20 | tf_op jit(solution)/shard_map/ppermute | solution.py:303
  70.6 3.6 %collective-permute-start.3 = (f32[]{:T(128)}, f32[]{:T(128)}, u32[]{:S(2)}, u32[]{:S(2)}) collective-permute-start(f32[]{:T(128)} %max.15), channel_id=1, source_target_pairs={{0,2},{1,3},{2,0},{3,1},{4,6},{5,7},{6,4},{7,5},{8,10},{9,11},{10,... | collective-permute-start | bytes 20 | tf_op jit(solution)/shard_map/ppermute | solution.py:303
  74.8 3.6 %collective-permute-start.4 = (f32[]{:T(128)}, f32[]{:T(128)}, u32[]{:S(2)}, u32[]{:S(2)}) collective-permute-start(f32[]{:T(128)} %max.16), channel_id=1, source_target_pairs={{0,4},{4,0},{8,12},{12,8},{16,20},{20,16},{24,28},{28,24},{1,5},{5... | collective-permute-start | bytes 20 | tf_op jit(solution)/shard_map/ppermute | solution.py:303
  79.0 3.6 %collective-permute-start.5 = (f32[]{:T(128)}, f32[]{:T(128)}, u32[]{:S(2)}, u32[]{:S(2)}) collective-permute-start(f32[]{:T(128)} %max.17), channel_id=1, source_target_pairs={{0,8},{4,12},{8,0},{12,4},{16,24},{20,28},{24,16},{28,20},{1,9},{5... | collective-permute-start | bytes 20 | tf_op jit(solution)/shard_map/ppermute | solution.py:303
  83.2 4.5 %collective-permute-start.6 = (f32[]{:T(128)}, f32[]{:T(128)}, u32[]{:S(2)}, u32[]{:S(2)}) collective-permute-start(f32[]{:T(128)} %max.18), channel_id=1, source_target_pairs={{0,16},{4,20},{8,24},{12,28},{16,0},{20,4},{24,8},{28,12},{1,17},{... | collective-permute-start | bytes 20 | tf_op jit(solution)/shard_map/ppermute | solution.py:303
where the time goes:
time: 89.9 us; the launch traced here: 89.5 us
  Pallas kernels  48.6 us (54%)
  starting transfers between devices  24.3 us (27%)
  waiting for transfers between devices  7.45 us (8%)
  between operations  5.73 us (6%)
  local copies, waits for them, and re-layouts  3.32 us (4%)
    pallas_call x1, Pallas kernels, pair_pass(): pl.pallas_call(functools.partial(pair_kernel, blocks, wall_blocks), out_s...  48.6 us
    ppermute x5, starting transfers between devices, swapped(): lax.ppermute(shard, axis, [(i, i ^ 1 << bit) for i in range(lax.axis_size...  14.2 us
    all_to_all x1, starting transfers between devices, per_device(): lax.all_to_all(sent, 'orb', 0, 0, axis_index_groups=groups if len(groups)...  7.38 us
    ppermute x1, waiting for transfers between devices, padded(): lax.ppermute(lax.slice_in_dim(block, 0, width, axis=dim), axis, backward)  3.15 us
    ppermute x5, waiting for transfers between devices, swapped(): lax.ppermute(shard, axis, [(i, i ^ 1 << bit) for i in range(lax.axis_size...  2.6 us
    gather x2, local copies, waits for them, and re-layouts, per_device(): sent = own_blocks[jnp.concatenate([own_slot, ghost_list], axis=0)[slots]]  1.84 us
  transfers between devices with their start and end apart: 8, of which 7 were waited for; matrix products, arithmetic and copies ran while one was open for 0% of the time, Pallas kernels for 0%

commit v1 on v0

--- a/solution.py
+++ b/solution.py
@@ -194,20 +194,11 @@
 
 
 def pair_kernel(
-    blocks, walls, own_ref, ghost_ref, wall_ref, pair_ref, wpair_ref, place_ref,
+    blocks, walls, own_ref, ghost_ref, wall_ref, pair_ref, wpair_ref,
     rate_ref, accel_ref, peak_ref, stage, src, mom, rho, wsrc, wmom, tgt,
-    acc_cubed, acc_blend, table,
+    acc_cubed, acc_blend,
 ):
     ghosts = ghost_ref.shape[0] // 8
-    per_mask = ghosts // 8
-    place = place_ref[0]
-    for c in range(blocks):
-        table[c] = c
-    for mask in range(1, 8):
-        for g in range(per_mask):
-            table[blocks + (mask - 1) * per_mask + g] = (
-                blocks + jnp.bitwise_xor(place, mask) * per_mask + g
-            )
     fluid_sources(own_ref, blocks, 0, stage, src, mom, rho)
     fluid_sources(ghost_ref, ghosts, blocks, stage, src, mom, rho)
     wall_sources(wall_ref, walls, stage, wsrc, wmom)
@@ -218,12 +209,12 @@
         target_rho = own_ref[pl.ds(b * 8 + 6, 1), :]
         total = jnp.zeros((3 * MOMENTS, 2 * LANES), jnp.float32)
         for k in range(pair_ref.shape[1]):
-            s = table[pair_ref[b, k]]
+            s = pair_ref[b, k]
             product = jnp.dot(src[s], target, preferred_element_type=jnp.float32)
             guarded, falloff, cubed = falloff_of(product[:, :LANES])
             approach = product[:, LANES:]
             spread = (guarded + shift) * (rho[s] + target_rho)
-            viscous = jnp.maximum(approach, 0.0) / spread
+            viscous = jnp.maximum(approach, 0.0) * pl.reciprocal(spread, approx=True)
             total += weighted(mom[s], cubed, cubed * (falloff + viscous))
         for k in range(wpair_ref.shape[1]):
             s = wpair_ref[b, k]
@@ -265,7 +256,7 @@
     peak_ref[...] = jnp.full(peak_ref.shape, jnp.sqrt(jnp.max(square)), jnp.float32)
 
 
-def pair_pass(own, ghosts, walls, pair_list, wall_pairs, place):
+def pair_pass(own, ghosts, walls, pair_list, wall_pairs):
     blocks = own.shape[0] // 8
     ghost_blocks = ghosts.shape[0] // 8
     wall_blocks = walls.shape[0] // 4
@@ -280,7 +271,7 @@
             jax.ShapeDtypeStruct((3, blocks * LANES), jnp.float32),
             jax.ShapeDtypeStruct((8, LANES), jnp.float32),
         ),
-        in_specs=[vmem, vmem, vmem, smem, smem, smem],
+        in_specs=[vmem, vmem, vmem, smem, smem],
         out_specs=(vmem, vmem, vmem),
         scratch_shapes=[
             pltpu.VMEM((ghost_blocks * FEATURES, LANES), jnp.float32),
@@ -292,11 +283,10 @@
             pltpu.VMEM((blocks, FEATURES, 2 * LANES), jnp.bfloat16),
             pltpu.VMEM((blocks * MOMENTS, LANES), jnp.float32),
             pltpu.VMEM((blocks * MOMENTS, LANES), jnp.float32),
-            pltpu.SMEM((total,), jnp.int32),
         ],
         compiler_params=pltpu.CompilerParams(vmem_limit_bytes=40 * 1024 * 1024),
         name="pair_pass",
-    )(own, ghosts, walls, pair_list, wall_pairs, place)
+    )(own, ghosts, walls, pair_list, wall_pairs)
 
 
 def swapped(shard, axis, bit):
@@ -320,13 +310,13 @@
     block_total = fluid_state.shape[1] // LANES
     own_blocks = jnp.transpose(fluid_state.reshape(8, block_total, LANES), (1, 0, 2))
     place = lax.axis_index("orb") % 8
-    slots = jnp.bitwise_xor(jnp.arange(8, dtype=jnp.int32), place)
-    own_slot = jnp.zeros((1, ghost_list.shape[1]), jnp.int32)
-    sent = own_blocks[jnp.concatenate([own_slot, ghost_list], axis=0)[slots]]
     groups = [list(range(g, g + 8)) for g in range(0, lax.axis_size("orb"), 8)]
-    landed = lax.all_to_all(
-        sent, "orb", 0, 0, axis_index_groups=groups if len(groups) > 1 else None
-    )
+    groups = groups if len(groups) > 1 else None
+    everyone = lax.all_gather(own_blocks, "orb", axis_index_groups=groups)
+    lists = lax.all_gather(ghost_list, "orb", axis_index_groups=groups)
+    partners = jnp.bitwise_xor(jnp.arange(8, dtype=jnp.int32), place)
+    chosen = lists[partners[1:], jnp.arange(7, dtype=jnp.int32)]
+    landed = everyone[partners[1:, None], chosen]
     alive = (
         (jnp.arange(LANES, dtype=jnp.int32)[None, :] < wall_count[:, None])
         .astype(jnp.float32)
@@ -341,12 +331,8 @@
         wall_cands.reshape(-1, LANES),
         pair_list,
         wall_pairs,
-        place.reshape(1),
     )
-    peak = local_peak[0, 0]
-    for axis in ("wall", "orb"):
-        for bit in range((lax.axis_size(axis) - 1).bit_length()):
-            peak = jnp.maximum(peak, swapped(peak, axis, bit))
+    peak = jnp.max(lax.all_gather(local_peak[:1], ("orb", "wall")))
     time_step = courant * jnp.sqrt(smoothing / (peak + 1e-06))
     return (rate.reshape(-1), acceleration, time_step)
 

time: 89.9 us -> 167 us (1.86)
  blocking collectives: 0 us -> 107 us
  starting transfers between devices: 24.3 us -> 3.64 us
  waiting for transfers between devices: 7.45 us -> 0.01 us
  between operations: 5.73 us -> 2.6 us
  other arithmetic: 0.13 us -> 2.98 us
    all_gather x0 -> x3, blocking collectives: none -> 107 us  [the longest x1 43.3 us: per_device(): peak = jnp.max(lax.all_gather(local_peak[:1], ('orb', 'wall')))]
    ppermute x5 -> x0, starting transfers between devices: 14.2 us -> none  [swapped(): lax.ppermute(shard, axis, [(i, i ^ 1 << bit) for i in range(lax.axis_size...]
    all_to_all x1 -> x0, starting transfers between devices: 7.38 us -> none  [per_device(): lax.all_to_all(sent, 'orb', 0, 0, axis_index_groups=groups if len(groups)...]
    ppermute x1, waiting for transfers between devices: 3.15 us -> 0.01 us  [padded(): lax.ppermute(lax.slice_in_dim(block, 0, width, axis=dim), axis, backward)]
    ppermute x5 -> x0, waiting for transfers between devices: 2.6 us -> none  [swapped(): lax.ppermute(shard, axis, [(i, i ^ 1 << bit) for i in range(lax.axis_size...]
    all_to_all x1 -> x0, waiting for transfers between devices: 1.7 us -> none  [per_device(): lax.all_to_all(sent, 'orb', 0, 0, axis_index_groups=groups if len(groups)...]
  transfers between devices with their start and end apart: 8 -> 2, of which waited for: 7 -> 0; matrix products, arithmetic and copies ran while one was open for 0% -> 1% of each run, Pallas kernels for 0% -> 0%
where the time goes in v1:
time: 167 us; the launch traced here: 166 us
  blocking collectives  107 us (64%)
  Pallas kernels  47.1 us (28%)
  starting transfers between devices  3.64 us (2%)
  other arithmetic  2.98 us (2%)
  local copies, waits for them, and re-layouts  2.76 us (2%)
  between operations  2.6 us (2%)
    pallas_call x1, Pallas kernels, pair_pass(): pl.pallas_call(functools.partial(pair_kernel, blocks, wall_blocks), out_s...  47.1 us
    all_gather x1, blocking collectives, per_device(): peak = jnp.max(lax.all_gather(local_peak[:1], ('orb', 'wall')))  43.3 us
    all_gather x1, blocking collectives, per_device(): everyone = lax.all_gather(own_blocks, 'orb', axis_index_groups=groups)  32.2 us
    all_gather x1, blocking collectives, per_device(): lists = lax.all_gather(ghost_list, 'orb', axis_index_groups=groups)  31.7 us
  transfers between devices with their start and end apart: 2, of which 0 were waited for; matrix products, arithmetic and copies ran while one was open for 1% of the time, Pallas kernels for 0%

profile of v1, /device:TPU:0, one launch (start us, length us, event | category | flops | bytes accessed | tf_op | source)
XLA Modules:
  0.0 166.4 jit_solution(3811584677990456547)
XLA Ops:
  0.6 0.0 copy-start
  0.6 0.8 fusion.3
  1.4 0.7 bitcast_select_fusion
  2.1 0.7 pad_maximum_fusion.2
  2.8 2.3 %collective-permute-start = (f32[4,128]{1,0:T(4,128)S(1)}, f32[4,128]{1,0:T(4,128)S(1)}, u32[]{:S(2)}, u32[]{:S(2)}) collective-permute-start(f32[4,128]{1,0:T(4,128)S(1)} %get-tuple-element.11), channel_id=1, source_target_pairs={{0,1},{1,2},{2,3},{4,5},{5,6},{6,7},{8,9},{9,10},{10,11},{12,13},{... | collective-permute-start | bytes 6152 | tf_op jit(solution)/shard_map/ppermute | solution.py:301
  5.2 1.3 collective-permute-start.1
  6.5 0.1 fusion.6
  6.6 31.7 %all-gather.3 = s32[8,7,6]{2,1,0:T(8,128)S(1)} all-gather(s32[1,7,6]{2,1,0:T(8,128)} %bitcast.39), channel_id=3, replica_groups=mesh['orb'=8,'wall'=4] {'orb'}, dimensions={0}, use_global_device_ids=true | all-gather | bytes 1512 | tf_op jit(solution)/shard_map/all_gather | solution.py:316
  38.3 0.0 copy-done
  38.3 32.2 %all-gather = f32[192,8,128]{2,1,0:T(8,128)S(1)} all-gather(f32[24,8,128]{2,1,0:T(8,128)S(1)} %bitcast.33), channel_id=2, replica_groups=mesh['orb'=8,'wall'=4] {'orb'}, dimensions={0}, use_global_device_ids=true | all-gather | bytes 884736 | tf_op jit(solution)/shard_map/all_gather | solution.py:315
  70.5 0.6 gather_fusion
  71.1 0.0 copy-start.2
  71.1 0.1 fusion.2
  71.2 0.1 reshape.77
  71.3 0.5 copy-done.2
  71.8 0.1 copy.19.pair_ref
  71.9 0.6 copy-done.3
  72.5 0.1 copy.20.wpair_ref
  72.6 0.8 gather_fusion.1
  73.4 0.0 collective-permute-done
  73.4 0.0 collective-permute-done.1
  73.4 47.1 %pair_pass.1 = (f32[24,128]{1,0:T(8,128)}, f32[3,3072]{1,0:T(4,128)}, f32[8,128]{1,0:T(8,128)S(1)}) custom-call(f32[192,128]{1,0:T(8,128)S(1)} %bitcast.34, f32[336,128]{1,0:T(8,128)S(1)} %bitcast.32, f32[32,128]{1,0:T(8,128)S(1)} %bitcast.35, s32[24,14]{1,0:T(8,128)S(1)} %copy.19.pair_ref, s32[24,4]{1,0:T(8,128)S(1)} %copy.20.wpair_ref), custom_call_target="tpu_custom_call" | custom-call | tf_op jit(solution)/shard_map/pair_pass/pallas_call | solution.py:267
  120.5 43.3 %all-gather.4 = f32[32,1,128]{2,1,0:T(1,128)S(1)} all-gather(f32[1,1,128]{2,1,0:T(1,128)S(1)} %slice_bitcast_fusion), channel_id=4, replica_groups=mesh['orb'=8,'wall'=4] {'orb','wall'}, dimensions={0}, use_global_device_ids=true | all-gather | bytes 16896 | tf_op jit(solution)/shard_map/all_gather | solution.py:335
  163.9 0.6 reduce
  (7 shorter events, 0.0 us)
Async XLA Ops:
  0.6 37.7 %copy-start = (f32[8,3072]{1,0:T(8,128)S(1)}, f32[8,3072]{1,0:T(8,128)}, u32[]{:S(2)}) copy-start(f32[8,3072]{1,0:T(8,128)} %param.6) | copy-start | bytes 294916
  2.8 70.6 %collective-permute-start = (f32[4,128]{1,0:T(4,128)S(1)}, f32[4,128]{1,0:T(4,128)S(1)}, u32[]{:S(2)}, u32[]{:S(2)}) collective-permute-start(f32[4,128]{1,0:T(4,128)S(1)} %get-tuple-element.11), channel_id=1, source_target_pairs={{0,1},{1,2},{2,3},{4,5},{5,6},{6,7},{8,9},{9,10},{10,11},{12,13},{... | collective-permute-start | bytes 6152 | tf_op jit(solution)/shard_map/ppermute | solution.py:301
  5.2 68.2 %collective-permute-start.1 = (f32[4,128]{1,0:T(4,128)S(1)}, f32[4,128]{1,0:T(4,128)S(1)}, u32[]{:S(2)}, u32[]{:S(2)}) collective-permute-start(f32[4,128]{1,0:T(4,128)S(1)} %get-tuple-element.12), channel_id=1, source_target_pairs={{1,0},{2,1},{3,2},{5,4},{6,5},{7,6},{9,8},{10,9},{11,10},{13,12},{... | collective-permute-start | bytes 6152 | tf_op jit(solution)/shard_map/ppermute | solution.py:304
  71.1 0.7 copy-start.2
  71.8 0.7 copy-start.3
  72.6 0.8 copy-start.1

commit v2 on v0

--- a/solution.py
+++ b/solution.py
@@ -11,6 +11,7 @@
 LANES = 128
 FEATURES = 64
 MOMENTS = 16
+CHUNK = 16
 
 smoothing = 0.1
 support = 0.3
@@ -180,64 +181,168 @@
     return guarded, falloff, falloff * falloff * falloff
 
 
-def weighted(moments, cubed, blend):
-    cubed_high, cubed_low = in_two(cubed)
-    blend_high, blend_low = in_two(blend)
-    weights = jnp.concatenate(
-        [
-            jnp.concatenate([cubed_high, blend_high], axis=1),
-            jnp.concatenate([cubed_low, blend_low], axis=1),
-        ],
-        axis=0,
-    )
-    return jnp.dot(moments, weights, preferred_element_type=jnp.float32)
-
-
-def pair_kernel(
-    blocks, walls, own_ref, ghost_ref, wall_ref, pair_ref, wpair_ref, place_ref,
-    rate_ref, accel_ref, peak_ref, stage, src, mom, rho, wsrc, wmom, tgt,
-    acc_cubed, acc_blend, table,
+def put_weights(weights, first, cubed, blend):
+    rows = cubed.shape[0]
+    for half, value in enumerate((cubed, blend)):
+        lanes = slice(half * LANES, (half + 1) * LANES)
+        high, low = in_two(value)
+        weights[first : first + rows, lanes] = high
+        weights[LANES + first : LANES + first + rows, lanes] = low
+
+
+def fluid_weights(product, weights, rho_j, rho_i):
+    for first in range(0, LANES, CHUNK):
+        rows = slice(first, first + CHUNK)
+        guarded, falloff, cubed = falloff_of(product[rows, :LANES])
+        spread = (guarded + shift) * (rho_j[rows, :] + rho_i)
+        viscous = jnp.maximum(product[rows, LANES:], 0.0) * pl.reciprocal(spread, approx=True)
+        put_weights(weights, first, cubed, cubed * (falloff + viscous))
+
+
+def wall_weights(product, weights):
+    for first in range(0, LANES, CHUNK):
+        _, falloff, cubed = falloff_of(product[first : first + CHUNK, :LANES])
+        put_weights(weights, first, cubed, cubed * falloff)
+
+
+def listed(pair_ref, keep, source_of, sources, targets, trash):
+    blocks, width = pair_ref.shape
+
+    def put(at, source, target):
+        sources[at] = source
+        targets[at] = target
+
+    put(0, 0, trash)
+
+    def row(b, count):
+        for k in range(width):
+            candidate = pair_ref[b, k]
+            put(count + 1, source_of(candidate), b)
+            count += keep(candidate)
+        return count
+
+    count = lax.fori_loop(0, blocks, row, 0)
+    for extra in range(1, 4):
+        put(count + extra, 0, trash)
+    return count
+
+
+def run_pairs(count, sources, targets, blocks, first, second, third):
+    def at(t):
+        target = targets[t + 1]
+        return sources[t + 1], jnp.minimum(target, blocks - 1), target
+
+    first(0, *at(0)[:2])
+
+    def steps(i, carry):
+        for slot in range(2):
+            t = 2 * i + slot
+            first(1 - slot, *at(t + 1)[:2])
+            second(slot, *at(t)[:2])
+            source, _, target = at(t - 1)
+            third(1 - slot, source, target)
+        return carry
+
+    pairs = (count + 1) // 2
+    lax.fori_loop(0, pairs, steps, 0)
+    source, _, target = at(2 * pairs - 1)
+    third(1, source, target)
+
+
+def stages(own_ref, src, mom, rho, tgt, acc, products, weights):
+    def first(slot, s, b):
+        if rho is not None:
+            products[slot][...] = jnp.dot(src[s], tgt[b], preferred_element_type=jnp.float32)
+        else:
+            products[slot][:, :LANES] = jnp.dot(
+                src[s], tgt[b, :, :LANES], preferred_element_type=jnp.float32
+            )
+
+    def second(slot, s, b):
+        if rho is not None:
+            rho_i = own_ref[pl.ds(b * 8 + 6, 1), :]
+            fluid_weights(products[slot], weights[slot], rho.at[s], rho_i)
+        else:
+            wall_weights(products[slot], weights[slot])
+
+    def third(slot, s, b):
+        acc[b] += jnp.dot(mom[s], weights[slot][...], preferred_element_type=jnp.float32)
+
+    return first, second, third
+
+
+def folded(acc, b):
+    total = acc[b]
+    return total[:MOMENTS] + total[MOMENTS : 2 * MOMENTS] + total[2 * MOMENTS :]
+
+
+def own_kernel(
+    blocks, own_ref, pair_ref, tgt, sum_cubed, sum_blend,
+    stage, src, mom, rho, acc, product0, product1, weight0, weight1, sources, targets,
+):
+    count = listed(
+        pair_ref, lambda c: (c < blocks).astype(jnp.int32), lambda c: jnp.minimum(c, blocks - 1),
+        sources, targets, blocks,
+    )
+    fluid_sources(own_ref, blocks, 0, stage, src, mom, rho)
+    put_targets(own_ref, blocks, stage, tgt)
+    acc[...] = jnp.zeros_like(acc)
+    parts = stages(
+        own_ref, src, mom, rho, tgt, acc, (product0, product1), (weight0, weight1)
+    )
+    run_pairs(count, sources, targets, blocks, *parts)
+
+    def fold(b, carry):
+        total = folded(acc, b)
+        rows = pl.ds(pl.multiple_of(b * MOMENTS, MOMENTS), MOMENTS)
+        sum_cubed[rows, :] = total[:, :LANES]
+        sum_blend[rows, :] = total[:, LANES:]
+        return carry
+
+    lax.fori_loop(0, blocks, fold, 0)
+
+
+def ghost_kernel(
+    blocks, walls, own_ref, ghost_ref, wall_ref, pair_ref, wpair_ref, place_ref, tgt, own_cubed,
+    own_blend, rate_ref, accel_ref, peak_ref, stage, src, mom, rho, wsrc, wmom, acc,
+    acc_cubed, acc_blend, product0, product1, weight0, weight1, sources, targets, wsources,
+    wtargets, table,
 ):
     ghosts = ghost_ref.shape[0] // 8
     per_mask = ghosts // 8
-    place = place_ref[0]
     for c in range(blocks):
-        table[c] = c
+        table[c] = 0
     for mask in range(1, 8):
         for g in range(per_mask):
             table[blocks + (mask - 1) * per_mask + g] = (
-                blocks + jnp.bitwise_xor(place, mask) * per_mask + g
+                jnp.bitwise_xor(place_ref[0], mask) * per_mask + g
             )
-    fluid_sources(own_ref, blocks, 0, stage, src, mom, rho)
-    fluid_sources(ghost_ref, ghosts, blocks, stage, src, mom, rho)
+    count = listed(
+        pair_ref, lambda c: (c >= blocks).astype(jnp.int32), lambda c: table[c],
+        sources, targets, blocks,
+    )
+    wcount = listed(wpair_ref, lambda c: 1, lambda c: c, wsources, wtargets, blocks)
+    fluid_sources(ghost_ref, ghosts, 0, stage, src, mom, rho)
     wall_sources(wall_ref, walls, stage, wsrc, wmom)
-    put_targets(own_ref, blocks, stage, tgt)
-
-    def per_target(b, carry):
-        target = tgt[b]
-        target_rho = own_ref[pl.ds(b * 8 + 6, 1), :]
-        total = jnp.zeros((3 * MOMENTS, 2 * LANES), jnp.float32)
-        for k in range(pair_ref.shape[1]):
-            s = table[pair_ref[b, k]]
-            product = jnp.dot(src[s], target, preferred_element_type=jnp.float32)
-            guarded, falloff, cubed = falloff_of(product[:, :LANES])
-            approach = product[:, LANES:]
-            spread = (guarded + shift) * (rho[s] + target_rho)
-            viscous = jnp.maximum(approach, 0.0) / spread
-            total += weighted(mom[s], cubed, cubed * (falloff + viscous))
-        for k in range(wpair_ref.shape[1]):
-            s = wpair_ref[b, k]
-            product = jnp.dot(wsrc[s], target[:, :LANES], preferred_element_type=jnp.float32)
-            _, falloff, cubed = falloff_of(product)
-            total += weighted(wmom[s], cubed, cubed * falloff)
-        folded = total[:MOMENTS] + total[MOMENTS : 2 * MOMENTS] + total[2 * MOMENTS :]
+    acc[...] = jnp.zeros_like(acc)
+    buffers = ((product0, product1), (weight0, weight1))
+    parts = stages(own_ref, src, mom, rho, tgt, acc, *buffers)
+    run_pairs(count, sources, targets, blocks, *parts)
+    parts = stages(own_ref, wsrc, wmom, None, tgt, acc, *buffers)
+    run_pairs(wcount, wsources, wtargets, blocks, *parts)
+
+    def fold(b, carry):
+        total = folded(acc, b)
         rows = pl.ds(pl.multiple_of(b * MOMENTS, MOMENTS), MOMENTS)
-        acc_cubed[rows, :] = folded[:, :LANES]
-        acc_blend[rows, :] = folded[:, LANES:]
+        acc_cubed[rows, :] = own_cubed[rows, :] + total[:, :LANES]
+        acc_blend[rows, :] = own_blend[rows, :] + total[:, LANES:]
         return carry
 
-    lax.fori_loop(0, blocks, per_target, 0)
-
+    lax.fori_loop(0, blocks, fold, 0)
+    finish(blocks, own_ref, acc_cubed, acc_blend, stage, rate_ref, accel_ref, peak_ref)
+
+
+def finish(blocks, own_ref, acc_cubed, acc_blend, stage, rate_ref, accel_ref, peak_ref):
     pos = scaled_position(own_ref, blocks, 8)
     vel = [loaded(own_ref, 3 + d, blocks, 8) for d in range(3)]
     own_press = grad_coeff * pressure_ratio(loaded(own_ref, 6, blocks, 8))
@@ -265,42 +370,84 @@
     peak_ref[...] = jnp.full(peak_ref.shape, jnp.sqrt(jnp.max(square)), jnp.float32)
 
 
-def pair_pass(own, ghosts, walls, pair_list, wall_pairs, place):
+def buffers_for(sources, blocks):
+    depth = 3 * MOMENTS
+    wide = pltpu.VMEM((LANES, 2 * LANES), jnp.float32)
+    square = pltpu.VMEM((2 * LANES, 2 * LANES), jnp.bfloat16)
+    return (
+        [
+            pltpu.VMEM((max(sources, blocks) * FEATURES, LANES), jnp.float32),
+            pltpu.VMEM((sources, LANES, FEATURES), jnp.bfloat16),
+            pltpu.VMEM((sources, depth, 2 * LANES), jnp.bfloat16),
+            pltpu.VMEM((sources, LANES, LANES), jnp.float32),
+        ],
+        pltpu.VMEM((blocks + 1, depth, 2 * LANES), jnp.float32),
+        [wide, wide, square, square],
+    )
+
+
+def tile_cost(tiles):
+    return pl.CostEstimate(
+        flops=tiles * LANES * LANES * 1000, bytes_accessed=0, transcendentals=0
+    )
+
+
+SMEM = pl.BlockSpec(memory_space=pltpu.SMEM)
+VMEM = pl.BlockSpec(memory_space=pltpu.VMEM)
+PARAMS = pltpu.CompilerParams(vmem_limit_bytes=40 * 1024 * 1024)
+
+
+def own_pass(own, pair_list):
+    blocks = own.shape[0] // 8
+    entries = pair_list.size + 4
+    sums = jax.ShapeDtypeStruct((blocks * MOMENTS, LANES), jnp.float32)
+    features, acc, buffers = buffers_for(blocks, blocks)
+    return pl.pallas_call(
+        functools.partial(own_kernel, blocks),
+        out_shape=(
+            jax.ShapeDtypeStruct((blocks, FEATURES, 2 * LANES), jnp.bfloat16), sums, sums,
+        ),
+        in_specs=[VMEM, SMEM],
+        out_specs=(VMEM, VMEM, VMEM),
+        scratch_shapes=features + [acc] + buffers + [pltpu.SMEM((entries,), jnp.int32)] * 2,
+        compiler_params=PARAMS,
+        cost_estimate=tile_cost(pair_list.size),
+        name="own_pass",
+    )(own, pair_list)
+
+
+def ghost_pass(own, ghosts, walls, pair_list, wall_pairs, place, tgt, cubed, blend):
     blocks = own.shape[0] // 8
     ghost_blocks = ghosts.shape[0] // 8
     wall_blocks = walls.shape[0] // 4
-    total = blocks + ghost_blocks
     depth = 3 * MOMENTS
-    smem = pl.BlockSpec(memory_space=pltpu.SMEM)
-    vmem = pl.BlockSpec(memory_space=pltpu.VMEM)
+    features, acc, buffers = buffers_for(ghost_blocks, blocks)
+    sums = pltpu.VMEM((blocks * MOMENTS, LANES), jnp.float32)
     return pl.pallas_call(
-        functools.partial(pair_kernel, blocks, wall_blocks),
+        functools.partial(ghost_kernel, blocks, wall_blocks),
         out_shape=(
             jax.ShapeDtypeStruct((blocks, LANES), jnp.float32),
             jax.ShapeDtypeStruct((3, blocks * LANES), jnp.float32),
             jax.ShapeDtypeStruct((8, LANES), jnp.float32),
         ),
-        in_specs=[vmem, vmem, vmem, smem, smem, smem],
-        out_specs=(vmem, vmem, vmem),
-        scratch_shapes=[
-            pltpu.VMEM((ghost_blocks * FEATURES, LANES), jnp.float32),
-            pltpu.VMEM((total, LANES, FEATURES), jnp.bfloat16),
-            pltpu.VMEM((total, depth, 2 * LANES), jnp.bfloat16),
-            pltpu.VMEM((total, LANES, LANES), jnp.float32),
+        in_specs=[VMEM, VMEM, VMEM, SMEM, SMEM, SMEM, VMEM, VMEM, VMEM],
+        out_specs=(VMEM, VMEM, VMEM),
+        scratch_shapes=features
+        + [
             pltpu.VMEM((wall_blocks, LANES, FEATURES), jnp.bfloat16),
             pltpu.VMEM((wall_blocks, depth, 2 * LANES), jnp.bfloat16),
-            pltpu.VMEM((blocks, FEATURES, 2 * LANES), jnp.bfloat16),
-            pltpu.VMEM((blocks * MOMENTS, LANES), jnp.float32),
-            pltpu.VMEM((blocks * MOMENTS, LANES), jnp.float32),
-            pltpu.SMEM((total,), jnp.int32),
-        ],
-        compiler_params=pltpu.CompilerParams(vmem_limit_bytes=40 * 1024 * 1024),
-        name="pair_pass",
-    )(own, ghosts, walls, pair_list, wall_pairs, place)
-
-
-def swapped(shard, axis, bit):
-    return lax.ppermute(shard, axis, [(i, i ^ 1 << bit) for i in range(lax.axis_size(axis))])
+            acc,
+            sums,
+            sums,
+        ]
+        + buffers
+        + [pltpu.SMEM((pair_list.size + 4,), jnp.int32)] * 2
+        + [pltpu.SMEM((wall_pairs.size + 4,), jnp.int32)] * 2
+        + [pltpu.SMEM((blocks + ghost_blocks,), jnp.int32)],
+        compiler_params=PARAMS,
+        cost_estimate=tile_cost(pair_list.size),
+        name="ghost_pass",
+    )(own, ghosts, walls, pair_list, wall_pairs, place, tgt, cubed, blend)
 
 
 def padded(block, sides, width):
@@ -320,9 +467,8 @@
     block_total = fluid_state.shape[1] // LANES
     own_blocks = jnp.transpose(fluid_state.reshape(8, block_total, LANES), (1, 0, 2))
     place = lax.axis_index("orb") % 8
-    slots = jnp.bitwise_xor(jnp.arange(8, dtype=jnp.int32), place)
-    own_slot = jnp.zeros((1, ghost_list.shape[1]), jnp.int32)
-    sent = own_blocks[jnp.concatenate([own_slot, ghost_list], axis=0)[slots]]
+    masks = jnp.bitwise_xor(jnp.arange(8, dtype=jnp.int32), place)
+    sent = own_blocks[ghost_list[jnp.maximum(masks - 1, 0)]]
     groups = [list(range(g, g + 8)) for g in range(0, lax.axis_size("orb"), 8)]
     landed = lax.all_to_all(
         sent, "orb", 0, 0, axis_index_groups=groups if len(groups) > 1 else None
@@ -335,18 +481,22 @@
     wall_live = jnp.concatenate([wall_state[0:3], wall_state[3:4] * alive[None, :]], axis=0)
     extended = padded(wall_live, (("wall", 1),), EB * LANES)
     wall_cands = jnp.transpose(extended.reshape(4, -1, LANES), (1, 0, 2))
-    rate, acceleration, local_peak = pair_pass(
-        own_blocks.reshape(-1, LANES),
+    own = own_blocks.reshape(-1, LANES)
+    own_sums = own_pass(own, pair_list)
+    rate, acceleration, local_peak = ghost_pass(
+        own,
         landed.reshape(-1, LANES),
         wall_cands.reshape(-1, LANES),
         pair_list,
         wall_pairs,
         place.reshape(1),
-    )
-    peak = local_peak[0, 0]
+        *own_sums,
+    )
+    peak = local_peak[:1]
     for axis in ("wall", "orb"):
-        for bit in range((lax.axis_size(axis) - 1).bit_length()):
-            peak = jnp.maximum(peak, swapped(peak, axis, bit))
+        copies = jnp.broadcast_to(peak, (lax.axis_size(axis), 1, LANES))
+        peak = jnp.max(lax.all_to_all(copies, axis, 0, 0), axis=0)
+    peak = peak[0, 0]
     time_step = courant * jnp.sqrt(smoothing / (peak + 1e-06))
     return (rate.reshape(-1), acceleration, time_step)
 

time: 89.9 us -> 111 us (1.23)
  Pallas kernels: 48.6 us -> 72 us
  blocking collectives: 0 us -> 21.1 us
  starting transfers between devices: 24.3 us -> 10.4 us
  waiting for transfers between devices: 7.45 us -> 0.01 us
  between operations: 5.73 us -> 2.01 us
  other arithmetic: 0.13 us -> 2.25 us
    pallas_call x1 -> x2, Pallas kernels: 48.6 us -> 72 us  [the longest x1 48.9 us: ghost_pass(): pl.pallas_call(functools.partial(ghost_kernel, blocks, wall_blocks), out_...]
    all_to_all x0 -> x2, blocking collectives: none -> 21.1 us  [per_device(): peak = jnp.max(lax.all_to_all(copies, axis, 0, 0), axis=0)]
    ppermute x5 -> x0, starting transfers between devices: 14.2 us -> none  [swapped(): lax.ppermute(shard, axis, [(i, i ^ 1 << bit) for i in range(lax.axis_size...]
    ppermute x1, waiting for transfers between devices: 3.15 us -> 0.01 us  [padded(): lax.ppermute(lax.slice_in_dim(block, 0, width, axis=dim), axis, backward)]
    ppermute x5 -> x0, waiting for transfers between devices: 2.6 us -> none  [swapped(): lax.ppermute(shard, axis, [(i, i ^ 1 << bit) for i in range(lax.axis_size...]
    all_to_all x1, waiting for transfers between devices: 1.7 us -> 0.01 us  [per_device(): lax.all_to_all(sent, 'orb', 0, 0, axis_index_groups=groups if len(groups)...]
  transfers between devices with their start and end apart: 8 -> 3, of which waited for: 7 -> 0; matrix products, arithmetic and copies ran while one was open for 0% -> 2% of each run, Pallas kernels for 0% -> 21%
where the time goes in v2:
time: 111 us
  Pallas kernels  72 us (65%)
  blocking collectives  21.1 us (19%)
  starting transfers between devices  10.4 us (9%)
  local copies, waits for them, and re-layouts  2.72 us (2%)
  other arithmetic  2.25 us (2%)
  between operations  2.01 us (2%)
    pallas_call x1, Pallas kernels, ghost_pass(): pl.pallas_call(functools.partial(ghost_kernel, blocks, wall_blocks), out_...  48.9 us
    pallas_call x1, Pallas kernels, own_pass(): pl.pallas_call(functools.partial(own_kernel, blocks), out_shape=(jax.Shap...  23.1 us
    all_to_all x2, blocking collectives, per_device(): peak = jnp.max(lax.all_to_all(copies, axis, 0, 0), axis=0)  21.1 us
    all_to_all x1, starting transfers between devices, per_device(): lax.all_to_all(sent, 'orb', 0, 0, axis_index_groups=groups if len(groups)...  6.77 us
    ppermute x1, starting transfers between devices, padded(): lax.ppermute(lax.slice_in_dim(block, block.shape[dim] - width, None, axis...  2.34 us
  transfers between devices with their start and end apart: 3, of which 0 were waited for; matrix products, arithmetic and copies ran while one was open for 2% of the time, Pallas kernels for 21%

profile of v2, /device:TPU:0, one launch (start us, length us, event | category | flops | bytes accessed | tf_op | source)
XLA Modules:
  0.0 110.5 jit_solution(17422361335025555939)
XLA Ops:
  0.6 0.0 copy-start
  0.6 0.0 copy-start.1
  0.7 0.8 fusion
  1.4 0.7 bitcast_select_fusion
  2.1 0.7 pad_maximum_fusion.2
  2.8 2.3 %collective-permute-start = (f32[4,128]{1,0:T(4,128)S(1)}, f32[4,128]{1,0:T(4,128)S(1)}, u32[]{:S(2)}, u32[]{:S(2)}) collective-permute-start(f32[4,128]{1,0:T(4,128)S(1)} %get-tuple-element.15), channel_id=1, source_target_pairs={{0,1},{1,2},{2,3},{4,5},{5,6},{6,7},{8,9},{9,10},{10,11},{12,13},{... | collective-permute-start | bytes 6152 | tf_op jit(solution)/shard_map/ppermute | solution.py:458
  5.2 1.3 %collective-permute-start.1 = (f32[4,128]{1,0:T(4,128)S(1)}, f32[4,128]{1,0:T(4,128)S(1)}, u32[]{:S(2)}, u32[]{:S(2)}) collective-permute-start(f32[4,128]{1,0:T(4,128)S(1)} %get-tuple-element.16), channel_id=1, source_target_pairs={{1,0},{2,1},{3,2},{5,4},{6,5},{7,6},{9,8},{10,9},{11,10},{13,12},{... | collective-permute-start | bytes 6152 | tf_op jit(solution)/shard_map/ppermute | solution.py:461
  6.5 0.0 copy-done
  6.5 0.6 gather_fusion
  7.1 0.1 reshape.105
  7.2 0.0 copy-done.1
  7.2 1.3 %gather_fusion.1 = f32[48,8,128]{2,1,0:T(8,128)} fusion(f32[24,8,128]{2,1,0:T(8,128)S(1)} %bitcast.33, s32[1024]{0:T(1024)S(1)} %pad_clamp_fusion), kind=kCustom, calls=%fused_computation.1 | custom fusion | bytes 393408 | tf_op jit(solution)/shard_map/gather | solution.py:471
  8.5 6.8 %all-to-all-start = ((f32[8,6,8,128]{3,2,1,0:T(8,128)}), f32[8,6,8,128]{3,2,1,0:T(8,128)S(1)}, u32[]{:S(2)}, u32[]{:S(2)}) async-start(f32[8,6,8,128]{3,2,1,0:T(8,128)} %bitcast.6), calls=%async_computation | async-start | bytes 393216 | tf_op jit(solution)/shard_map/all_to_all | solution.py:473
  15.3 0.1 copy.23.pair_ref
  15.3 23.1 %own_pass.1 = (bf16[24,64,256]{2,1,0:T(8,128)(2,1)S(1)}, f32[384,128]{1,0:T(8,128)S(1)}, f32[384,128]{1,0:T(8,128)S(1)}) custom-call(f32[192,128]{1,0:T(8,128)S(1)} %bitcast.34, s32[24,14]{1,0:T(8,128)S(1)} %copy.23.pair_ref), custom_call_target="tpu_custom_call" | custom-call | flops 5505024000 | tf_op jit(solution)/shard_map/own_pass/pallas_call | solution.py:405
  38.5 0.0 copy-start.2
  38.5 0.1 copy.24.wpair_ref
  38.6 0.0 collective-permute-done
  38.6 0.0 collective-permute-done.1
  38.6 0.6 copy-done.2
  39.2 0.0 all-to-all-done
  39.2 48.9 %ghost_pass.1 = (f32[24,128]{1,0:T(8,128)}, f32[3,3072]{1,0:T(4,128)}, f32[8,128]{1,0:T(8,128)S(1)}) custom-call(f32[192,128]{1,0:T(8,128)S(1)} %bitcast.35, f32[384,128]{1,0:T(8,128)S(1)} %bitcast.36, f32[32,128]{1,0:T(8,128)S(1)} %bitcast.37, s32[24,14]{1,0:T(8,128)S(1)} %copy.23.pair_ref, s32[24,4]{1,0:T(8,128)S(1)} %copy.24.wpair_ref, ...), custom_call_target="tpu_custom_call" | custom-call | flops 5505024000 | tf_op jit(solution)/shard_map/ghost_pass/pallas_call | solution.py:426
  88.1 8.7 %all_to_all.15 = f32[4,1,128]{2,1,0:T(1,128)S(1)} all-to-all(f32[4,1,128]{2,1,0:T(1,128)S(1)} %broadcast_in_dim.4), channel_id=1, replica_groups=mesh['orb'=8,'wall'=4] {'wall'}, dimensions={0} | all-to-all | bytes 4096 | tf_op jit(solution)/shard_map/all_to_all | solution.py:498
  96.8 12.5 %all_to_all.16 = f32[8,1,128]{2,1,0:T(1,128)S(1)} all-to-all(f32[8,1,128]{2,1,0:T(1,128)S(1)} %broadcast_in_dim.5), channel_id=1, replica_groups=mesh['orb'=8,'wall'=4] {'orb'}, dimensions={0} | all-to-all | bytes 8192 | tf_op jit(solution)/shard_map/all_to_all | solution.py:498
  (14 shorter events, 0.1 us)
Async XLA Ops:
  0.6 5.9 %copy-start = (s32[7,6]{1,0:T(8,128)S(1)}, s32[7,6]{1,0:T(8,128)}, u32[]{:S(2)}) copy-start(s32[7,6]{1,0:T(8,128)} %param.7) | copy-start | bytes 508
  0.6 6.6 %copy-start.1 = (f32[8,3072]{1,0:T(8,128)S(1)}, f32[8,3072]{1,0:T(8,128)}, u32[]{:S(2)}) copy-start(f32[8,3072]{1,0:T(8,128)} %param.6) | copy-start | bytes 294916
  2.8 35.7 %collective-permute-start = (f32[4,128]{1,0:T(4,128)S(1)}, f32[4,128]{1,0:T(4,128)S(1)}, u32[]{:S(2)}, u32[]{:S(2)}) collective-permute-start(f32[4,128]{1,0:T(4,128)S(1)} %get-tuple-element.15), channel_id=1, source_target_pairs={{0,1},{1,2},{2,3},{4,5},{5,6},{6,7},{8,9},{9,10},{10,11},{12,13},{... | collective-permute-start | bytes 6152 | tf_op jit(solution)/shard_map/ppermute | solution.py:458
  5.2 33.4 %collective-permute-start.1 = (f32[4,128]{1,0:T(4,128)S(1)}, f32[4,128]{1,0:T(4,128)S(1)}, u32[]{:S(2)}, u32[]{:S(2)}) collective-permute-start(f32[4,128]{1,0:T(4,128)S(1)} %get-tuple-element.16), channel_id=1, source_target_pairs={{1,0},{2,1},{3,2},{5,4},{6,5},{7,6},{9,8},{10,9},{11,10},{13,12},{... | collective-permute-start | bytes 6152 | tf_op jit(solution)/shard_map/ppermute | solution.py:461
  8.5 6.8 %copy-start.3 = (s32[24,14]{0,1:T(8,128)S(1)}, s32[24,14]{0,1:T(8,128)}, u32[]{:S(2)}) copy-start(s32[24,14]{0,1:T(8,128)} %param.8) | copy-start | bytes 4036
  8.5 30.7 %all-to-all-start = ((f32[8,6,8,128]{3,2,1,0:T(8,128)}), f32[8,6,8,128]{3,2,1,0:T(8,128)S(1)}, u32[]{:S(2)}, u32[]{:S(2)}) async-start(f32[8,6,8,128]{3,2,1,0:T(8,128)} %bitcast.6), calls=%async_computation | async-start | bytes 393216 | tf_op jit(solution)/shard_map/all_to_all | solution.py:473
  15.3 23.1 %copy-start.4 = (s32[24,4]{0,1:T(4,128)S(1)}, s32[24,4]{0,1:T(4,128)}, u32[]{:S(2)}) copy-start(s32[24,4]{0,1:T(4,128)} %param.11) | copy-start | bytes 1156
  38.5 0.7 copy-start.2

commit v3 on v0

v3 whole, which is shorter than its diff:
```python
import functools

import jax
import jax.numpy as jnp
from jax import lax
from jax.experimental import pallas as pl
from jax.experimental.pallas import tpu as pltpu
from jax.sharding import PartitionSpec as P

EB = 1
LANES = 128
FEATURES = 64
MOMENTS = 16
CHUNK = 16

smoothing = 0.1
support = 0.3
kernel_norm = 21.0 / (2.0 * 3.141592653589793 * support**3)
grad_coeff = -20.0 / support**2 * kernel_norm
tait_coeff = 25.0 / 7.0
visc_coeff = 0.05
cohesion = 2000.0
adhesion = 2000.0
gravity = 9.81
courant = 0.25

center = 0.3
shift = 0.0001 / support**2
approach_coeff = grad_coeff * visc_coeff * 2.0 / (support * 4.0 * cohesion)
press_coeff = -grad_coeff / (4.0 * cohesion)

SPLITS = ((0, 0), (0, 1), (1, 0), (0, 2), (2, 0), (1, 1), (1, 2), (2, 1))


def rounded(value):
    return value.astype(jnp.bfloat16).astype(jnp.float32)


def split(value):
    first = rounded(value)
    rest = value - first
    second = rounded(rest)
    return (first, second, rest - second)


def dotted(left, right):
    return left[0] * right[0] + left[1] * right[1] + left[2] * right[2]


def pressure_ratio(density):
    square = density * density
    return tait_coeff * (square * square * square * density - 1.0) / square


def loaded(ref, row, count, stride):
    return ref[pl.ds(row, count, stride=stride), :]


def scaled_position(ref, count, stride):
    return [(loaded(ref, d, count, stride) - center) * (1.0 / support) for d in range(3)]


def source_rows(pos, vel, extras):
    one = jnp.ones_like(pos[0])
    zero = one * 0.0
    rows = [one, one, one]
    rows += split(dotted(pos, pos))
    rows += split(approach_coeff * dotted(pos, vel)) if vel is not None else [zero] * 3
    for part in (pos, vel) if vel is not None else (pos,):
        for value in part:
            pieces = split(value)
            rows += [pieces[t] for _, t in SPLITS]
    return rows + [zero] * (FEATURES - len(rows) - len(extras)) + extras


def target_rows(pos, vel):
    one = jnp.ones_like(pos[0])
    zero = one * 0.0
    near = list(split(dotted(pos, pos))) + [one] * 3 + [zero] * 3
    along = list(split(approach_coeff * dotted(pos, vel))) + [zero] * 3 + [one] * 3
    for d in range(3):
        pieces = split(-2.0 * pos[d])
        near += [pieces[p] for p, _ in SPLITS]
        pieces = split(-approach_coeff * vel[d])
        along += [pieces[p] for p, _ in SPLITS]
    for d in range(3):
        pieces = split(-approach_coeff * pos[d])
        along += [pieces[p] for p, _ in SPLITS]
    near += [zero] * (FEATURES - len(near))
    along += [zero] * (FEATURES - len(along))
    return near, along


def moment_rows(pos, mass):
    pieces = [split(column) for column in [mass] + [mass * p for p in pos]]
    rows = [piece[p] for p in range(3) for piece in pieces]
    return rows + [mass * 0.0] * (MOMENTS - len(rows))


def put_sources(rows, moments, count, base, extras, stage, src, mom, wide):
    for k, row in enumerate(rows):
        stage[pl.ds(k, count, stride=FEATURES), :] = row

    def turn(b, carry):
        block = stage[pl.ds(pl.multiple_of(b * FEATURES, FEATURES), FEATURES), :]
        turned = block.T
        src[base + b] = turned.astype(jnp.bfloat16)
        for n in range(extras):
            lane = FEATURES - extras + n
            wide[base + b, n] = jnp.broadcast_to(turned[:, lane : lane + 1], (LANES, LANES))
        return carry

    lax.fori_loop(0, count, turn, 0)
    for k, row in enumerate(moments):
        stage[pl.ds(k, count, stride=MOMENTS), :] = row

    def place(b, carry):
        block = stage[pl.ds(pl.multiple_of(b * MOMENTS, MOMENTS), MOMENTS), :]
        mom[base + b] = block.astype(jnp.bfloat16)
        return carry

    lax.fori_loop(0, count, place, 0)


def fluid_sources(ref, count, base, stage, src, mom, wide):
    pos = scaled_position(ref, count, 8)
    vel = [loaded(ref, 3 + d, count, 8) for d in range(3)]
    density = loaded(ref, 6, count, 8)
    mass = loaded(ref, 7, count, 8)
    extras = [mass, density, press_coeff * pressure_ratio(density) - 0.75]
    rows = source_rows(pos, vel, extras)
    put_sources(rows, moment_rows(pos, mass), count, base, 3, stage, src, mom, wide)


def wall_sources(ref, count, stage, src, mom, wide):
    pos = scaled_position(ref, count, 4)
    mass = loaded(ref, 3, count, 4)
    rows = source_rows(pos, None, [mass])
    moments = moment_rows(pos, (adhesion / cohesion) * mass)
    put_sources(rows, moments, count, 0, 1, stage, src, mom, wide)


def put_targets(ref, count, stage, tgt):
    pos = scaled_position(ref, count, 8)
    vel = [loaded(ref, 3 + d, count, 8) for d in range(3)]
    for half, rows in enumerate(target_rows(pos, vel)):
        for k, row in enumerate(rows):
            stage[pl.ds(k, count, stride=FEATURES), :] = row

        def place(b, carry):
            block = stage[pl.ds(pl.multiple_of(b * FEATURES, FEATURES), FEATURES), :]
            tgt[b, :, half * LANES : (half + 1) * LANES] = block.astype(jnp.bfloat16)
            return carry

        lax.fori_loop(0, count, place, 0)


def in_two(value):
    high = value.astype(jnp.bfloat16)
    return high, (value - high.astype(jnp.float32)).astype(jnp.bfloat16)


def falloff_of(dist_sq):
    guarded = jnp.maximum(dist_sq, 1e-30)
    root = guarded * lax.rsqrt(guarded)
    falloff = jnp.maximum(1.0 - root, 0.0)
    return guarded, falloff, falloff * falloff * falloff


def weights_of(product, press_i, rho_i, wide):
    highs, lows = [], []
    rate = jnp.zeros((8, LANES), jnp.float32)
    for first in range(0, LANES, CHUNK):
        rows = slice(first, first + CHUNK)
        approach = product[rows, LANES:]
        guarded, falloff, cubed = falloff_of(product[rows, :LANES])
        blend = falloff + press_i
        if rho_i is not None:
            spread = (guarded + shift) * (wide[1, rows, :] + rho_i)
            blend += wide[2, rows, :]
            blend += jnp.maximum(approach, 0.0) * pl.reciprocal(spread, approx=True)
        high, low = in_two(cubed * blend)
        highs.append(high)
        lows.append(low)
        part = (cubed * approach) * wide[0, rows, :]
        for n in range(0, CHUNK, 8):
            rate += part[n : n + 8]
    halves = [jnp.concatenate(pieces, axis=0) for pieces in (highs, lows)]
    return jnp.concatenate(halves, axis=1), rate


def pair_kernel(
    blocks, walls, own_ref, ghost_ref, wall_ref, pair_ref, wpair_ref, place_ref,
    rate_ref, accel_ref, peak_ref, stage, src, mom, wide, wsrc, wmom, wwide, tgt, press, sums,
    rates, table,
):
    ghosts = ghost_ref.shape[0] // 8
    per_mask = ghosts // 8
    for c in range(blocks):
        table[c] = c
    for mask in range(1, 8):
        for g in range(per_mask):
            table[blocks + (mask - 1) * per_mask + g] = (
                blocks + jnp.bitwise_xor(place_ref[0], mask) * per_mask + g
            )
    fluid_sources(own_ref, blocks, 0, stage, src, mom, wide)
    fluid_sources(ghost_ref, ghosts, blocks, stage, src, mom, wide)
    wall_sources(wall_ref, walls, stage, wsrc, wmom, wwide)
    put_targets(own_ref, blocks, stage, tgt)
    press[...] = press_coeff * pressure_ratio(loaded(own_ref, 6, blocks, 8))

    def per_target(b, carry):
        target = tgt[b]
        rho_i = own_ref[pl.ds(b * 8 + 6, 1), :]
        press_i = press[pl.ds(b, 1), :]
        wall_press = (2.0 * cohesion / adhesion) * press_i - 0.75
        tiles = []
        for k in range(pair_ref.shape[1]):
            s = table[pair_ref[b, k]]
            tiles.append((src.at[s], mom.at[s], wide.at[s], press_i, rho_i))
        for k in range(wpair_ref.shape[1]):
            s = wpair_ref[b, k]
            tiles.append((wsrc.at[s], wmom.at[s], wwide.at[s], wall_press, None))

        def product_of(tile):
            return jnp.dot(tile[0][...], target, preferred_element_type=jnp.float32)

        total = jnp.zeros((MOMENTS, 2 * LANES), jnp.float32)
        rate = jnp.zeros((8, LANES), jnp.float32)
        ahead = product_of(tiles[0])
        waiting = None
        for n, (_, moments, spread, tile_press, tile_rho) in enumerate(tiles):
            product = ahead
            if n + 1 < len(tiles):
                ahead = product_of(tiles[n + 1])
            weights, part = weights_of(product, tile_press, tile_rho, spread)
            rate += part
            if waiting is not None:
                total += jnp.dot(*waiting, preferred_element_type=jnp.float32)
            waiting = (moments[...], weights)
        total += jnp.dot(*waiting, preferred_element_type=jnp.float32)
        rows = pl.ds(pl.multiple_of(b * MOMENTS, MOMENTS), MOMENTS)
        sums[rows, :] = total[:, :LANES] + total[:, LANES:]
        rates[pl.ds(pl.multiple_of(b * 8, 8), 8), :] = rate
        return carry

    lax.fori_loop(0, blocks, per_target, 0)

    pos = scaled_position(own_ref, blocks, 8)
    rate = loaded(rates, 0, blocks, 8)
    for n in range(1, 8):
        rate += loaded(rates, n, blocks, 8)
    rate_ref[...] = (support * grad_coeff / approach_coeff) * rate

    def summed(column):
        parts = [loaded(sums, p * 4 + column, blocks, MOMENTS) for p in range(3)]
        return parts[0] + parts[1] + parts[2]

    mass_sum = summed(0)
    square = jnp.zeros_like(rate)
    for d in range(3):
        force = (4.0 * cohesion * support) * (pos[d] * mass_sum - summed(1 + d))
        if d == 2:
            force -= gravity
        square += force * force
        stage[pl.ds(d, blocks, stride=8), :] = force
    for b in range(blocks):
        accel_ref[:, b * LANES : (b + 1) * LANES] = stage[b * 8 : b * 8 + 3, :]
    peak_ref[...] = jnp.full(peak_ref.shape, jnp.sqrt(jnp.max(square)), jnp.float32)


def pair_pass(own, ghosts, walls, pair_list, wall_pairs, place):
    blocks = own.shape[0] // 8
    ghost_blocks = ghosts.shape[0] // 8
    wall_blocks = walls.shape[0] // 4
    total = blocks + ghost_blocks
    smem = pl.BlockSpec(memory_space=pltpu.SMEM)
    vmem = pl.BlockSpec(memory_space=pltpu.VMEM)
    return pl.pallas_call(
        functools.partial(pair_kernel, blocks, wall_blocks),
        out_shape=(
            jax.ShapeDtypeStruct((blocks, LANES), jnp.float32),
            jax.ShapeDtypeStruct((3, blocks * LANES), jnp.float32),
            jax.ShapeDtypeStruct((8, LANES), jnp.float32),
        ),
        in_specs=[vmem, vmem, vmem, smem, smem, smem],
        out_specs=(vmem, vmem, vmem),
        scratch_shapes=[
            pltpu.VMEM((ghost_blocks * FEATURES, LANES), jnp.float32),
            pltpu.VMEM((total, LANES, FEATURES), jnp.bfloat16),
            pltpu.VMEM((total, MOMENTS, LANES), jnp.bfloat16),
            pltpu.VMEM((total, 3, LANES, LANES), jnp.float32),
            pltpu.VMEM((wall_blocks, LANES, FEATURES), jnp.bfloat16),
            pltpu.VMEM((wall_blocks, MOMENTS, LANES), jnp.bfloat16),
            pltpu.VMEM((wall_blocks, 1, LANES, LANES), jnp.float32),
            pltpu.VMEM((blocks, FEATURES, 2 * LANES), jnp.bfloat16),
            pltpu.VMEM((blocks, LANES), jnp.float32),
            pltpu.VMEM((blocks * MOMENTS, LANES), jnp.float32),
            pltpu.VMEM((blocks * 8, LANES), jnp.float32),
            pltpu.SMEM((total,), jnp.int32),
        ],
        compiler_params=pltpu.CompilerParams(vmem_limit_bytes=40 * 1024 * 1024),
        name="pair_pass",
    )(own, ghosts, walls, pair_list, wall_pairs, place)


def swapped(shard, axis, bit):
    return lax.ppermute(shard, axis, [(i, i ^ 1 << bit) for i in range(lax.axis_size(axis))])


def padded(block, sides, width):
    for axis, dim in sides:
        count = lax.axis_size(axis)
        forward = [(i, i + 1) for i in range(count - 1)]
        backward = [(target, source) for source, target in forward]
        low = lax.ppermute(
            lax.slice_in_dim(block, block.shape[dim] - width, None, axis=dim), axis, forward
        )
        high = lax.ppermute(lax.slice_in_dim(block, 0, width, axis=dim), axis, backward)
        block = jnp.concatenate([low, block, high], axis=dim)
    return block


def per_device(fluid_state, ghost_list, pair_list, wall_state, wall_count, wall_pairs):
    block_total = fluid_state.shape[1] // LANES
    own_blocks = jnp.transpose(fluid_state.reshape(8, block_total, LANES), (1, 0, 2))
    place = lax.axis_index("orb") % 8
    masks = jnp.bitwise_xor(jnp.arange(8, dtype=jnp.int32), place)
    sent = own_blocks[ghost_list[jnp.maximum(masks - 1, 0)]]
    groups = [list(range(g, g + 8)) for g in range(0, lax.axis_size("orb"), 8)]
    landed = lax.all_to_all(
        sent, "orb", 0, 0, axis_index_groups=groups if len(groups) > 1 else None
    )
    alive = (
        (jnp.arange(LANES, dtype=jnp.int32)[None, :] < wall_count[:, None])
        .astype(jnp.float32)
        .reshape(-1)
    )
    wall_live = jnp.concatenate([wall_state[0:3], wall_state[3:4] * alive[None, :]], axis=0)
    extended = padded(wall_live, (("wall", 1),), EB * LANES)
    wall_cands = jnp.transpose(extended.reshape(4, -1, LANES), (1, 0, 2))
    rate, acceleration, local_peak = pair_pass(
        own_blocks.reshape(-1, LANES),
        landed.reshape(-1, LANES),
        wall_cands.reshape(-1, LANES),
        pair_list,
        wall_pairs,
        place.reshape(1),
    )
    peak = local_peak
    for axis in ("wall", "orb"):
        for bit in range((lax.axis_size(axis) - 1).bit_length()):
            peak = jnp.maximum(peak, swapped(peak, axis, bit))
    peak = peak[0, 0]
    time_step = courant * jnp.sqrt(smoothing / (peak + 1e-06))
    return (rate.reshape(-1), acceleration, time_step)


def solution(mesh):
    return jax.shard_map(
        per_device,
        mesh=mesh,
        in_specs=(
            P(None, ("orb", "wall")),
            P(None, ("orb", "wall")),
            P(("orb", "wall"), None),
            P(None, ("orb", "wall")),
            P(("orb", "wall")),
            P(("orb", "wall"), None),
        ),
        out_specs=(P(("orb", "wall")), P(None, ("orb", "wall")), P()),
        check_vma=False,
    )
```

time: 89.9 us -> 94.8 us (1.055)
  Pallas kernels: 48.6 us -> 55.7 us
  waiting for transfers between devices: 7.45 us -> 12.8 us
  starting transfers between devices: 24.3 us -> 19 us
  between operations: 5.73 us -> 2.6 us
    pallas_call x1, Pallas kernels: 48.6 us -> 55.7 us  [pair_pass(): pl.pallas_call(functools.partial(pair_kernel, blocks, wall_blocks), out_s...]
    ppermute x5, waiting for transfers between devices: 2.6 us -> 7.98 us  [swapped(): lax.ppermute(shard, axis, [(i, i ^ 1 << bit) for i in range(lax.axis_size...]
    ppermute x5, starting transfers between devices: 14.2 us -> 8.82 us  [swapped(): lax.ppermute(shard, axis, [(i, i ^ 1 << bit) for i in range(lax.axis_size...]
where the time goes in v3:
time: 94.8 us; the launch traced here: 94.4 us
  Pallas kernels  55.7 us (59%)
  starting transfers between devices  19 us (20%)
  waiting for transfers between devices  12.8 us (14%)
  local copies, waits for them, and re-layouts  4.13 us (4%)
  between operations  2.6 us (3%)
    pallas_call x1, Pallas kernels, pair_pass(): pl.pallas_call(functools.partial(pair_kernel, blocks, wall_blocks), out_s...  55.7 us
    ppermute x5, starting transfers between devices, swapped(): lax.ppermute(shard, axis, [(i, i ^ 1 << bit) for i in range(lax.axis_size...  8.82 us
    ppermute x5, waiting for transfers between devices, swapped(): lax.ppermute(shard, axis, [(i, i ^ 1 << bit) for i in range(lax.axis_size...  7.98 us
    all_to_all x1, starting transfers between devices, per_device(): lax.all_to_all(sent, 'orb', 0, 0, axis_index_groups=groups if len(groups)...  7.4 us
    ppermute x1, waiting for transfers between devices, padded(): lax.ppermute(lax.slice_in_dim(block, 0, width, axis=dim), axis, backward)  3.15 us
    gather x2, local copies, waits for them, and re-layouts, per_device(): sent = own_blocks[ghost_list[jnp.maximum(masks - 1, 0)]]  2.7 us
  transfers between devices with their start and end apart: 8, of which 7 were waited for; matrix products, arithmetic and copies ran while one was open for 0% of the time, Pallas kernels for 0%

profile of v3, /device:TPU:0, one launch (start us, length us, event | category | flops | bytes accessed | tf_op | source)
XLA Modules:
  0.0 94.4 jit_solution(16185125203900809124)
XLA Ops:
  0.7 0.6 copy-done
  1.3 0.6 gather_fusion
  1.9 0.1 reshape.100
  2.0 2.2 %gather_fusion.1 = f32[48,8,128]{2,1,0:T(8,128)} fusion(f32[24,8,128]{2,1,0:T(8,128)} %bitcast.27, s32[1024]{0:T(1024)S(1)} %pad_clamp_fusion), kind=kCustom, calls=%fused_computation.1 | custom fusion | bytes 393408 | tf_op jit(solution)/shard_map/gather | solution.py:329
  4.1 7.4 %all-to-all-start = ((f32[8,6,8,128]{3,2,1,0:T(8,128)}), f32[8,6,8,128]{3,2,1,0:T(8,128)S(1)}, u32[]{:S(2)}, u32[]{:S(2)}) async-start(f32[8,6,8,128]{3,2,1,0:T(8,128)} %bitcast.6), calls=%async_computation | async-start | bytes 393216 | tf_op jit(solution)/shard_map/all_to_all | solution.py:331
  11.6 0.1 fusion
  11.7 1.5 %collective-permute-start = (f32[4,128]{1,0:T(4,128)S(1)}, f32[4,128]{1,0:T(4,128)S(1)}, u32[]{:S(2)}, u32[]{:S(2)}) collective-permute-start(f32[4,128]{1,0:T(4,128)S(1)} %get-tuple-element.9), channel_id=1, source_target_pairs={{0,1},{1,2},{2,3},{4,5},{5,6},{6,7},{8,9},{9,10},{10,11},{12,13},{... | collective-permute-start | bytes 6152 | tf_op jit(solution)/shard_map/ppermute | solution.py:316
  13.1 1.3 %collective-permute-start.1 = (f32[4,128]{1,0:T(4,128)S(1)}, f32[4,128]{1,0:T(4,128)S(1)}, u32[]{:S(2)}, u32[]{:S(2)}) collective-permute-start(f32[4,128]{1,0:T(4,128)S(1)} %get-tuple-element.10), channel_id=1, source_target_pairs={{1,0},{2,1},{3,2},{5,4},{6,5},{7,6},{9,8},{10,9},{11,10},{13,12},{... | collective-permute-start | bytes 6152 | tf_op jit(solution)/shard_map/ppermute | solution.py:319
  14.4 0.1 copy.13.pair_ref
  14.5 0.1 copy.14.wpair_ref
  14.6 3.2 %collective-permute-done.1 = f32[4,128]{1,0:T(4,128)S(1)} collective-permute-done((f32[4,128]{1,0:T(4,128)S(1)}, f32[4,128]{1,0:T(4,128)S(1)}, u32[]{:S(2)}, u32[]{:S(2)}) %collective-permute-start.1) | collective-permute-done | bytes 2080 | tf_op jit(solution)/shard_map/ppermute | solution.py:319
  17.8 1.7 %all-to-all-done = f32[8,6,8,128]{3,2,1,0:T(8,128)S(1)} async-done(((f32[8,6,8,128]{3,2,1,0:T(8,128)}), f32[8,6,8,128]{3,2,1,0:T(8,128)S(1)}, u32[]{:S(2)}, u32[]{:S(2)}) %all-to-all-start) | async-done | bytes 196640 | tf_op jit(solution)/shard_map/all_to_all | solution.py:331
  19.5 55.7 %pair_pass.1 = (f32[24,128]{1,0:T(8,128)}, f32[3,3072]{1,0:T(4,128)}, f32[8,128]{1,0:T(8,128)S(1)}) custom-call(f32[192,128]{1,0:T(8,128)S(1)} %bitcast.28, f32[384,128]{1,0:T(8,128)S(1)} %bitcast.29, f32[32,128]{1,0:T(8,128)S(1)} %bitcast.30, s32[24,14]{1,0:T(8,128)S(1)} %copy.13.pair_ref, s32[24,4]{1,0:T(8,128)S(1)} %copy.14.wpair_ref, s32[1]{0:T(128)} %bitcast.11.place_ref), custom_call_target="tpu_custom_call" | custom-call | tf_op jit(solution)/shard_map/pair_pass/pallas_call | solution.py:279
  75.2 0.6 collective-permute-start.2
  75.9 0.8 collective-permute-done.2
  76.7 1.2 %collective-permute-start.3 = (f32[8,128]{1,0:T(8,128)S(1)}, f32[8,128]{1,0:T(8,128)S(1)}, u32[]{:S(2)}, u32[]{:S(2)}) collective-permute-start(f32[8,128]{1,0:T(8,128)S(1)} %max.26), channel_id=1, source_target_pairs={{0,2},{1,3},{2,0},{3,1},{4,6},{5,7},{6,4},{7,5},{8,10},{9,11},{10,... | collective-permute-start | bytes 12296 | tf_op jit(solution)/shard_map/ppermute | solution.py:308
  77.9 2.4 %collective-permute-done.3 = f32[8,128]{1,0:T(8,128)S(1)} collective-permute-done((f32[8,128]{1,0:T(8,128)S(1)}, f32[8,128]{1,0:T(8,128)S(1)}, u32[]{:S(2)}, u32[]{:S(2)}) %collective-permute-start.3) | collective-permute-done | bytes 4128 | tf_op jit(solution)/shard_map/ppermute | solution.py:308
  80.3 2.0 %collective-permute-start.4 = (f32[8,128]{1,0:T(8,128)S(1)}, f32[8,128]{1,0:T(8,128)S(1)}, u32[]{:S(2)}, u32[]{:S(2)}) collective-permute-start(f32[8,128]{1,0:T(8,128)S(1)} %max.27), channel_id=1, source_target_pairs={{0,4},{4,0},{8,12},{12,8},{16,20},{20,16},{24,28},{28,24},{1,5},{5... | collective-permute-start | bytes 12296 | tf_op jit(solution)/shard_map/ppermute | solution.py:308
  82.3 1.6 %collective-permute-done.4 = f32[8,128]{1,0:T(8,128)S(1)} collective-permute-done((f32[8,128]{1,0:T(8,128)S(1)}, f32[8,128]{1,0:T(8,128)S(1)}, u32[]{:S(2)}, u32[]{:S(2)}) %collective-permute-start.4) | collective-permute-done | bytes 4128 | tf_op jit(solution)/shard_map/ppermute | solution.py:308
  83.9 2.0 %collective-permute-start.5 = (f32[8,128]{1,0:T(8,128)S(1)}, f32[8,128]{1,0:T(8,128)S(1)}, u32[]{:S(2)}, u32[]{:S(2)}) collective-permute-start(f32[8,128]{1,0:T(8,128)S(1)} %max.28), channel_id=1, source_target_pairs={{0,8},{4,12},{8,0},{12,4},{16,24},{20,28},{24,16},{28,20},{1,9},{5... | collective-permute-start | bytes 12296 | tf_op jit(solution)/shard_map/ppermute | solution.py:308
  85.9 1.6 %collective-permute-done.5 = f32[8,128]{1,0:T(8,128)S(1)} collective-permute-done((f32[8,128]{1,0:T(8,128)S(1)}, f32[8,128]{1,0:T(8,128)S(1)}, u32[]{:S(2)}, u32[]{:S(2)}) %collective-permute-start.5) | collective-permute-done | bytes 4128 | tf_op jit(solution)/shard_map/ppermute | solution.py:308
  87.5 2.9 %collective-permute-start.6 = (f32[8,128]{1,0:T(8,128)S(1)}, f32[8,128]{1,0:T(8,128)S(1)}, u32[]{:S(2)}, u32[]{:S(2)}) collective-permute-start(f32[8,128]{1,0:T(8,128)S(1)} %max.29), channel_id=1, source_target_pairs={{0,16},{4,20},{8,24},{12,28},{16,0},{20,4},{24,8},{28,12},{1,17},{... | collective-permute-start | bytes 12296 | tf_op jit(solution)/shard_map/ppermute | solution.py:308
  90.4 1.6 %collective-permute-done.6 = f32[8,128]{1,0:T(8,128)S(1)} collective-permute-done((f32[8,128]{1,0:T(8,128)S(1)}, f32[8,128]{1,0:T(8,128)S(1)}, u32[]{:S(2)}, u32[]{:S(2)}) %collective-permute-start.6) | collective-permute-done | bytes 4128 | tf_op jit(solution)/shard_map/ppermute | solution.py:308
  92.0 0.5 slice.19
  (24 shorter events, 0.1 us)
Async XLA Ops:
  0.6 0.7 copy-start
  4.1 7.4 %copy-start.5 = (s32[6]{0:T(128)S(1)}, s32[6]{0:T(128)}, u32[]{:S(2)}) copy-start(s32[6]{0:T(128)} %param.10) | copy-start | bytes 76
  4.1 7.5 %copy-start.2 = (f32[4,768]{1,0:T(4,128)S(1)}, f32[4,768]{1,0:T(4,128)}, u32[]{:S(2)}) copy-start(f32[4,768]{1,0:T(4,128)} %param.9) | copy-start | bytes 36868
  4.1 10.3 %copy-start.3 = (s32[24,14]{0,1:T(8,128)S(1)}, s32[24,14]{0,1:T(8,128)}, u32[]{:S(2)}) copy-start(s32[24,14]{0,1:T(8,128)} %param.8) | copy-start | bytes 4036
  4.1 10.4 %copy-start.4 = (s32[24,4]{0,1:T(4,128)S(1)}, s32[24,4]{0,1:T(4,128)}, u32[]{:S(2)}) copy-start(s32[24,4]{0,1:T(4,128)} %param.11) | copy-start | bytes 1156
  4.1 15.3 %all-to-all-start = ((f32[8,6,8,128]{3,2,1,0:T(8,128)}), f32[8,6,8,128]{3,2,1,0:T(8,128)S(1)}, u32[]{:S(2)}, u32[]{:S(2)}) async-start(f32[8,6,8,128]{3,2,1,0:T(8,128)} %bitcast.6), calls=%async_computation | async-start | bytes 393216 | tf_op jit(solution)/shard_map/all_to_all | solution.py:331
  11.5 8.0 %copy-start.1 = (f32[8,3072]{1,0:T(8,128)S(1)}, f32[8,3072]{1,0:T(8,128)}, u32[]{:S(2)}) copy-start(f32[8,3072]{1,0:T(8,128)} %param.6) | copy-start | bytes 294916
  11.7 3.0 %collective-permute-start = (f32[4,128]{1,0:T(4,128)S(1)}, f32[4,128]{1,0:T(4,128)S(1)}, u32[]{:S(2)}, u32[]{:S(2)}) collective-permute-start(f32[4,128]{1,0:T(4,128)S(1)} %get-tuple-element.9), channel_id=1, source_target_pairs={{0,1},{1,2},{2,3},{4,5},{5,6},{6,7},{8,9},{9,10},{10,11},{12,13},{... | collective-permute-start | bytes 6152 | tf_op jit(solution)/shard_map/ppermute | solution.py:316
  13.1 4.6 %collective-permute-start.1 = (f32[4,128]{1,0:T(4,128)S(1)}, f32[4,128]{1,0:T(4,128)S(1)}, u32[]{:S(2)}, u32[]{:S(2)}) collective-permute-start(f32[4,128]{1,0:T(4,128)S(1)} %get-tuple-element.10), channel_id=1, source_target_pairs={{1,0},{2,1},{3,2},{5,4},{6,5},{7,6},{9,8},{10,9},{11,10},{13,12},{... | collective-permute-start | bytes 6152 | tf_op jit(solution)/shard_map/ppermute | solution.py:319
  75.2 1.5 %collective-permute-start.2 = (f32[8,128]{1,0:T(8,128)S(1)}, f32[8,128]{1,0:T(8,128)S(1)}, u32[]{:S(2)}, u32[]{:S(2)}) collective-permute-start(f32[8,128]{1,0:T(8,128)S(1)} %get-tuple-element.8), channel_id=1, source_target_pairs={{0,1},{1,0},{2,3},{3,2},{4,5},{5,4},{6,7},{7,6},{8,9},{9,8},{10,11... | collective-permute-start | bytes 12296 | tf_op jit(solution)/shard_map/ppermute | solution.py:308
  76.7 3.6 %collective-permute-start.3 = (f32[8,128]{1,0:T(8,128)S(1)}, f32[8,128]{1,0:T(8,128)S(1)}, u32[]{:S(2)}, u32[]{:S(2)}) collective-permute-start(f32[8,128]{1,0:T(8,128)S(1)} %max.26), channel_id=1, source_target_pairs={{0,2},{1,3},{2,0},{3,1},{4,6},{5,7},{6,4},{7,5},{8,10},{9,11},{10,... | collective-permute-start | bytes 12296 | tf_op jit(solution)/shard_map/ppermute | solution.py:308
  80.3 3.6 %collective-permute-start.4 = (f32[8,128]{1,0:T(8,128)S(1)}, f32[8,128]{1,0:T(8,128)S(1)}, u32[]{:S(2)}, u32[]{:S(2)}) collective-permute-start(f32[8,128]{1,0:T(8,128)S(1)} %max.27), channel_id=1, source_target_pairs={{0,4},{4,0},{8,12},{12,8},{16,20},{20,16},{24,28},{28,24},{1,5},{5... | collective-permute-start | bytes 12296 | tf_op jit(solution)/shard_map/ppermute | solution.py:308
  83.9 3.6 %collective-permute-start.5 = (f32[8,128]{1,0:T(8,128)S(1)}, f32[8,128]{1,0:T(8,128)S(1)}, u32[]{:S(2)}, u32[]{:S(2)}) collective-permute-start(f32[8,128]{1,0:T(8,128)S(1)} %max.28), channel_id=1, source_target_pairs={{0,8},{4,12},{8,0},{12,4},{16,24},{20,28},{24,16},{28,20},{1,9},{5... | collective-permute-start | bytes 12296 | tf_op jit(solution)/shard_map/ppermute | solution.py:308
  87.5 4.5 %collective-permute-start.6 = (f32[8,128]{1,0:T(8,128)S(1)}, f32[8,128]{1,0:T(8,128)S(1)}, u32[]{:S(2)}, u32[]{:S(2)}) collective-permute-start(f32[8,128]{1,0:T(8,128)S(1)} %max.29), channel_id=1, source_target_pairs={{0,16},{4,20},{8,24},{12,28},{16,0},{20,4},{24,8},{28,12},{1,17},{... | collective-permute-start | bytes 12296 | tf_op jit(solution)/shard_map/ppermute | solution.py:308

commit v4 on v3

--- a/solution.py
+++ b/solution.py
@@ -11,7 +11,7 @@
 LANES = 128
 FEATURES = 64
 MOMENTS = 16
-CHUNK = 16
+CHUNK = 128
 
 smoothing = 0.1
 support = 0.3

time: 94.8 us -> 94.8 us (level)
  no operation moved by 1% of the time
where the time goes in v4:
time: 94.8 us; the launch traced here: 94.4 us
  Pallas kernels  55.7 us (59%)
  starting transfers between devices  19 us (20%)
  waiting for transfers between devices  12.8 us (14%)
  local copies, waits for them, and re-layouts  4.13 us (4%)
  between operations  2.6 us (3%)
    pallas_call x1, Pallas kernels, pair_pass(): pl.pallas_call(functools.partial(pair_kernel, blocks, wall_blocks), out_s...  55.7 us
    ppermute x5, starting transfers between devices, swapped(): lax.ppermute(shard, axis, [(i, i ^ 1 << bit) for i in range(lax.axis_size...  8.83 us
    ppermute x5, waiting for transfers between devices, swapped(): lax.ppermute(shard, axis, [(i, i ^ 1 << bit) for i in range(lax.axis_size...  7.98 us
    all_to_all x1, starting transfers between devices, per_device(): lax.all_to_all(sent, 'orb', 0, 0, axis_index_groups=groups if len(groups)...  7.4 us
    ppermute x1, waiting for transfers between devices, padded(): lax.ppermute(lax.slice_in_dim(block, 0, width, axis=dim), axis, backward)  3.15 us
    gather x2, local copies, waits for them, and re-layouts, per_device(): sent = own_blocks[ghost_list[jnp.maximum(masks - 1, 0)]]  2.7 us
  transfers between devices with their start and end apart: 8, of which 7 were waited for; matrix products, arithmetic and copies ran while one was open for 0% of the time, Pallas kernels for 0%

profile of v4, /device:TPU:0, one launch (start us, length us, event | category | flops | bytes accessed | tf_op | source)
XLA Modules:
  0.0 94.4 jit_solution(12845742169908496318)
XLA Ops:
  0.7 0.6 copy-done
  1.3 0.6 gather_fusion
  1.9 0.1 reshape.100
  2.0 2.2 %gather_fusion.1 = f32[48,8,128]{2,1,0:T(8,128)} fusion(f32[24,8,128]{2,1,0:T(8,128)} %bitcast.27, s32[1024]{0:T(1024)S(1)} %pad_clamp_fusion), kind=kCustom, calls=%fused_computation.1 | custom fusion | bytes 393408 | tf_op jit(solution)/shard_map/gather | solution.py:329
  4.1 7.4 %all-to-all-start = ((f32[8,6,8,128]{3,2,1,0:T(8,128)}), f32[8,6,8,128]{3,2,1,0:T(8,128)S(1)}, u32[]{:S(2)}, u32[]{:S(2)}) async-start(f32[8,6,8,128]{3,2,1,0:T(8,128)} %bitcast.6), calls=%async_computation | async-start | bytes 393216 | tf_op jit(solution)/shard_map/all_to_all | solution.py:331
  11.6 0.1 fusion
  11.7 1.5 %collective-permute-start = (f32[4,128]{1,0:T(4,128)S(1)}, f32[4,128]{1,0:T(4,128)S(1)}, u32[]{:S(2)}, u32[]{:S(2)}) collective-permute-start(f32[4,128]{1,0:T(4,128)S(1)} %get-tuple-element.9), channel_id=1, source_target_pairs={{0,1},{1,2},{2,3},{4,5},{5,6},{6,7},{8,9},{9,10},{10,11},{12,13},{... | collective-permute-start | bytes 6152 | tf_op jit(solution)/shard_map/ppermute | solution.py:316
  13.1 1.3 %collective-permute-start.1 = (f32[4,128]{1,0:T(4,128)S(1)}, f32[4,128]{1,0:T(4,128)S(1)}, u32[]{:S(2)}, u32[]{:S(2)}) collective-permute-start(f32[4,128]{1,0:T(4,128)S(1)} %get-tuple-element.10), channel_id=1, source_target_pairs={{1,0},{2,1},{3,2},{5,4},{6,5},{7,6},{9,8},{10,9},{11,10},{13,12},{... | collective-permute-start | bytes 6152 | tf_op jit(solution)/shard_map/ppermute | solution.py:319
  14.4 0.1 copy.13.pair_ref
  14.5 0.1 copy.14.wpair_ref
  14.6 3.2 %collective-permute-done.1 = f32[4,128]{1,0:T(4,128)S(1)} collective-permute-done((f32[4,128]{1,0:T(4,128)S(1)}, f32[4,128]{1,0:T(4,128)S(1)}, u32[]{:S(2)}, u32[]{:S(2)}) %collective-permute-start.1) | collective-permute-done | bytes 2080 | tf_op jit(solution)/shard_map/ppermute | solution.py:319
  17.8 1.7 %all-to-all-done = f32[8,6,8,128]{3,2,1,0:T(8,128)S(1)} async-done(((f32[8,6,8,128]{3,2,1,0:T(8,128)}), f32[8,6,8,128]{3,2,1,0:T(8,128)S(1)}, u32[]{:S(2)}, u32[]{:S(2)}) %all-to-all-start) | async-done | bytes 196640 | tf_op jit(solution)/shard_map/all_to_all | solution.py:331
  19.5 55.7 %pair_pass.1 = (f32[24,128]{1,0:T(8,128)}, f32[3,3072]{1,0:T(4,128)}, f32[8,128]{1,0:T(8,128)S(1)}) custom-call(f32[192,128]{1,0:T(8,128)S(1)} %bitcast.28, f32[384,128]{1,0:T(8,128)S(1)} %bitcast.29, f32[32,128]{1,0:T(8,128)S(1)} %bitcast.30, s32[24,14]{1,0:T(8,128)S(1)} %copy.13.pair_ref, s32[24,4]{1,0:T(8,128)S(1)} %copy.14.wpair_ref, s32[1]{0:T(128)} %bitcast.11.place_ref), custom_call_target="tpu_custom_call" | custom-call | tf_op jit(solution)/shard_map/pair_pass/pallas_call | solution.py:279
  75.2 0.6 collective-permute-start.2
  75.9 0.8 collective-permute-done.2
  76.7 1.2 %collective-permute-start.3 = (f32[8,128]{1,0:T(8,128)S(1)}, f32[8,128]{1,0:T(8,128)S(1)}, u32[]{:S(2)}, u32[]{:S(2)}) collective-permute-start(f32[8,128]{1,0:T(8,128)S(1)} %max.26), channel_id=1, source_target_pairs={{0,2},{1,3},{2,0},{3,1},{4,6},{5,7},{6,4},{7,5},{8,10},{9,11},{10,... | collective-permute-start | bytes 12296 | tf_op jit(solution)/shard_map/ppermute | solution.py:308
  77.9 2.4 %collective-permute-done.3 = f32[8,128]{1,0:T(8,128)S(1)} collective-permute-done((f32[8,128]{1,0:T(8,128)S(1)}, f32[8,128]{1,0:T(8,128)S(1)}, u32[]{:S(2)}, u32[]{:S(2)}) %collective-permute-start.3) | collective-permute-done | bytes 4128 | tf_op jit(solution)/shard_map/ppermute | solution.py:308
  80.3 2.0 %collective-permute-start.4 = (f32[8,128]{1,0:T(8,128)S(1)}, f32[8,128]{1,0:T(8,128)S(1)}, u32[]{:S(2)}, u32[]{:S(2)}) collective-permute-start(f32[8,128]{1,0:T(8,128)S(1)} %max.27), channel_id=1, source_target_pairs={{0,4},{4,0},{8,12},{12,8},{16,20},{20,16},{24,28},{28,24},{1,5},{5... | collective-permute-start | bytes 12296 | tf_op jit(solution)/shard_map/ppermute | solution.py:308
  82.3 1.6 %collective-permute-done.4 = f32[8,128]{1,0:T(8,128)S(1)} collective-permute-done((f32[8,128]{1,0:T(8,128)S(1)}, f32[8,128]{1,0:T(8,128)S(1)}, u32[]{:S(2)}, u32[]{:S(2)}) %collective-permute-start.4) | collective-permute-done | bytes 4128 | tf_op jit(solution)/shard_map/ppermute | solution.py:308
  83.9 2.0 %collective-permute-start.5 = (f32[8,128]{1,0:T(8,128)S(1)}, f32[8,128]{1,0:T(8,128)S(1)}, u32[]{:S(2)}, u32[]{:S(2)}) collective-permute-start(f32[8,128]{1,0:T(8,128)S(1)} %max.28), channel_id=1, source_target_pairs={{0,8},{4,12},{8,0},{12,4},{16,24},{20,28},{24,16},{28,20},{1,9},{5... | collective-permute-start | bytes 12296 | tf_op jit(solution)/shard_map/ppermute | solution.py:308
  85.9 1.6 %collective-permute-done.5 = f32[8,128]{1,0:T(8,128)S(1)} collective-permute-done((f32[8,128]{1,0:T(8,128)S(1)}, f32[8,128]{1,0:T(8,128)S(1)}, u32[]{:S(2)}, u32[]{:S(2)}) %collective-permute-start.5) | collective-permute-done | bytes 4128 | tf_op jit(solution)/shard_map/ppermute | solution.py:308
  87.5 2.9 %collective-permute-start.6 = (f32[8,128]{1,0:T(8,128)S(1)}, f32[8,128]{1,0:T(8,128)S(1)}, u32[]{:S(2)}, u32[]{:S(2)}) collective-permute-start(f32[8,128]{1,0:T(8,128)S(1)} %max.29), channel_id=1, source_target_pairs={{0,16},{4,20},{8,24},{12,28},{16,0},{20,4},{24,8},{28,12},{1,17},{... | collective-permute-start | bytes 12296 | tf_op jit(solution)/shard_map/ppermute | solution.py:308
  90.4 1.6 %collective-permute-done.6 = f32[8,128]{1,0:T(8,128)S(1)} collective-permute-done((f32[8,128]{1,0:T(8,128)S(1)}, f32[8,128]{1,0:T(8,128)S(1)}, u32[]{:S(2)}, u32[]{:S(2)}) %collective-permute-start.6) | collective-permute-done | bytes 4128 | tf_op jit(solution)/shard_map/ppermute | solution.py:308
  92.0 0.5 slice.19
  (24 shorter events, 0.1 us)
Async XLA Ops:
  0.6 0.7 copy-start
  4.1 7.4 %copy-start.5 = (s32[6]{0:T(128)S(1)}, s32[6]{0:T(128)}, u32[]{:S(2)}) copy-start(s32[6]{0:T(128)} %param.10) | copy-start | bytes 76
  4.1 7.5 %copy-start.2 = (f32[4,768]{1,0:T(4,128)S(1)}, f32[4,768]{1,0:T(4,128)}, u32[]{:S(2)}) copy-start(f32[4,768]{1,0:T(4,128)} %param.9) | copy-start | bytes 36868
  4.1 10.3 %copy-start.3 = (s32[24,14]{0,1:T(8,128)S(1)}, s32[24,14]{0,1:T(8,128)}, u32[]{:S(2)}) copy-start(s32[24,14]{0,1:T(8,128)} %param.8) | copy-start | bytes 4036
  4.1 10.4 %copy-start.4 = (s32[24,4]{0,1:T(4,128)S(1)}, s32[24,4]{0,1:T(4,128)}, u32[]{:S(2)}) copy-start(s32[24,4]{0,1:T(4,128)} %param.11) | copy-start | bytes 1156
  4.1 15.3 %all-to-all-start = ((f32[8,6,8,128]{3,2,1,0:T(8,128)}), f32[8,6,8,128]{3,2,1,0:T(8,128)S(1)}, u32[]{:S(2)}, u32[]{:S(2)}) async-start(f32[8,6,8,128]{3,2,1,0:T(8,128)} %bitcast.6), calls=%async_computation | async-start | bytes 393216 | tf_op jit(solution)/shard_map/all_to_all | solution.py:331
  11.5 8.0 %copy-start.1 = (f32[8,3072]{1,0:T(8,128)S(1)}, f32[8,3072]{1,0:T(8,128)}, u32[]{:S(2)}) copy-start(f32[8,3072]{1,0:T(8,128)} %param.6) | copy-start | bytes 294916
  11.7 3.0 %collective-permute-start = (f32[4,128]{1,0:T(4,128)S(1)}, f32[4,128]{1,0:T(4,128)S(1)}, u32[]{:S(2)}, u32[]{:S(2)}) collective-permute-start(f32[4,128]{1,0:T(4,128)S(1)} %get-tuple-element.9), channel_id=1, source_target_pairs={{0,1},{1,2},{2,3},{4,5},{5,6},{6,7},{8,9},{9,10},{10,11},{12,13},{... | collective-permute-start | bytes 6152 | tf_op jit(solution)/shard_map/ppermute | solution.py:316
  13.1 4.6 %collective-permute-start.1 = (f32[4,128]{1,0:T(4,128)S(1)}, f32[4,128]{1,0:T(4,128)S(1)}, u32[]{:S(2)}, u32[]{:S(2)}) collective-permute-start(f32[4,128]{1,0:T(4,128)S(1)} %get-tuple-element.10), channel_id=1, source_target_pairs={{1,0},{2,1},{3,2},{5,4},{6,5},{7,6},{9,8},{10,9},{11,10},{13,12},{... | collective-permute-start | bytes 6152 | tf_op jit(solution)/shard_map/ppermute | solution.py:319
  75.2 1.5 %collective-permute-start.2 = (f32[8,128]{1,0:T(8,128)S(1)}, f32[8,128]{1,0:T(8,128)S(1)}, u32[]{:S(2)}, u32[]{:S(2)}) collective-permute-start(f32[8,128]{1,0:T(8,128)S(1)} %get-tuple-element.8), channel_id=1, source_target_pairs={{0,1},{1,0},{2,3},{3,2},{4,5},{5,4},{6,7},{7,6},{8,9},{9,8},{10,11... | collective-permute-start | bytes 12296 | tf_op jit(solution)/shard_map/ppermute | solution.py:308
  76.7 3.6 %collective-permute-start.3 = (f32[8,128]{1,0:T(8,128)S(1)}, f32[8,128]{1,0:T(8,128)S(1)}, u32[]{:S(2)}, u32[]{:S(2)}) collective-permute-start(f32[8,128]{1,0:T(8,128)S(1)} %max.26), channel_id=1, source_target_pairs={{0,2},{1,3},{2,0},{3,1},{4,6},{5,7},{6,4},{7,5},{8,10},{9,11},{10,... | collective-permute-start | bytes 12296 | tf_op jit(solution)/shard_map/ppermute | solution.py:308
  80.3 3.6 %collective-permute-start.4 = (f32[8,128]{1,0:T(8,128)S(1)}, f32[8,128]{1,0:T(8,128)S(1)}, u32[]{:S(2)}, u32[]{:S(2)}) collective-permute-start(f32[8,128]{1,0:T(8,128)S(1)} %max.27), channel_id=1, source_target_pairs={{0,4},{4,0},{8,12},{12,8},{16,20},{20,16},{24,28},{28,24},{1,5},{5... | collective-permute-start | bytes 12296 | tf_op jit(solution)/shard_map/ppermute | solution.py:308
  83.9 3.6 %collective-permute-start.5 = (f32[8,128]{1,0:T(8,128)S(1)}, f32[8,128]{1,0:T(8,128)S(1)}, u32[]{:S(2)}, u32[]{:S(2)}) collective-permute-start(f32[8,128]{1,0:T(8,128)S(1)} %max.28), channel_id=1, source_target_pairs={{0,8},{4,12},{8,0},{12,4},{16,24},{20,28},{24,16},{28,20},{1,9},{5... | collective-permute-start | bytes 12296 | tf_op jit(solution)/shard_map/ppermute | solution.py:308
  87.5 4.5 %collective-permute-start.6 = (f32[8,128]{1,0:T(8,128)S(1)}, f32[8,128]{1,0:T(8,128)S(1)}, u32[]{:S(2)}, u32[]{:S(2)}) collective-permute-start(f32[8,128]{1,0:T(8,128)S(1)} %max.29), channel_id=1, source_target_pairs={{0,16},{4,20},{8,24},{12,28},{16,0},{20,4},{24,8},{28,12},{1,17},{... | collective-permute-start | bytes 12296 | tf_op jit(solution)/shard_map/ppermute | solution.py:308

commit v5 on v4

--- a/solution.py
+++ b/solution.py
@@ -110,7 +110,7 @@
             wide[base + b, n] = jnp.broadcast_to(turned[:, lane : lane + 1], (LANES, LANES))
         return carry
 
-    lax.fori_loop(0, count, turn, 0)
+    lax.fori_loop(0, count, turn, 0, unroll=8)
     for k, row in enumerate(moments):
         stage[pl.ds(k, count, stride=MOMENTS), :] = row
 
@@ -119,7 +119,7 @@
         mom[base + b] = block.astype(jnp.bfloat16)
         return carry
 
-    lax.fori_loop(0, count, place, 0)
+    lax.fori_loop(0, count, place, 0, unroll=8)
 
 
 def fluid_sources(ref, count, base, stage, src, mom, wide):
@@ -152,7 +152,7 @@
             tgt[b, :, half * LANES : (half + 1) * LANES] = block.astype(jnp.bfloat16)
             return carry
 
-        lax.fori_loop(0, count, place, 0)
+        lax.fori_loop(0, count, place, 0, unroll=8)
 
 
 def in_two(value):

time: 94.8 us -> 82.6 us (0.87)
  Pallas kernels: 55.7 us -> 43.5 us
    pallas_call x1, Pallas kernels: 55.7 us -> 43.5 us  [pair_pass(): pl.pallas_call(functools.partial(pair_kernel, blocks, wall_blocks), out_s...]
where the time goes in v5:
time: 82.6 us; the launch traced here: 82.2 us
  Pallas kernels  43.5 us (53%)
  starting transfers between devices  18.9 us (23%)
  waiting for transfers between devices  12.9 us (16%)
  local copies, waits for them, and re-layouts  4.13 us (5%)
  between operations  2.6 us (3%)
    pallas_call x1, Pallas kernels, pair_pass(): pl.pallas_call(functools.partial(pair_kernel, blocks, wall_blocks), out_s...  43.5 us
    ppermute x5, starting transfers between devices, swapped(): lax.ppermute(shard, axis, [(i, i ^ 1 << bit) for i in range(lax.axis_size...  8.78 us
    ppermute x5, waiting for transfers between devices, swapped(): lax.ppermute(shard, axis, [(i, i ^ 1 << bit) for i in range(lax.axis_size...  8.03 us
    all_to_all x1, starting transfers between devices, per_device(): lax.all_to_all(sent, 'orb', 0, 0, axis_index_groups=groups if len(groups)...  7.4 us
    ppermute x1, waiting for transfers between devices, padded(): lax.ppermute(lax.slice_in_dim(block, 0, width, axis=dim), axis, backward)  3.15 us
    gather x2, local copies, waits for them, and re-layouts, per_device(): sent = own_blocks[ghost_list[jnp.maximum(masks - 1, 0)]]  2.7 us
    all_to_all x1, waiting for transfers between devices, per_device(): lax.all_to_all(sent, 'orb', 0, 0, axis_index_groups=groups if len(groups)...  1.71 us
  transfers between devices with their start and end apart: 8, of which 7 were waited for; matrix products, arithmetic and copies ran while one was open for 0% of the time, Pallas kernels for 0%

profile of v5, /device:TPU:0, one launch (start us, length us, event | category | flops | bytes accessed | tf_op | source)
XLA Modules:
  0.0 82.2 jit_solution(1580989098589411048)
XLA Ops:
  0.7 0.6 copy-done
  1.3 0.6 gather_fusion
  1.9 0.1 reshape.100
  2.0 2.2 %gather_fusion.1 = f32[48,8,128]{2,1,0:T(8,128)} fusion(f32[24,8,128]{2,1,0:T(8,128)} %bitcast.27, s32[1024]{0:T(1024)S(1)} %pad_clamp_fusion), kind=kCustom, calls=%fused_computation.1 | custom fusion | bytes 393408 | tf_op jit(solution)/shard_map/gather | solution.py:329
  4.1 7.4 %all-to-all-start = ((f32[8,6,8,128]{3,2,1,0:T(8,128)}), f32[8,6,8,128]{3,2,1,0:T(8,128)S(1)}, u32[]{:S(2)}, u32[]{:S(2)}) async-start(f32[8,6,8,128]{3,2,1,0:T(8,128)} %bitcast.6), calls=%async_computation | async-start | bytes 393216 | tf_op jit(solution)/shard_map/all_to_all | solution.py:331
  11.6 0.1 fusion
  11.7 1.5 %collective-permute-start = (f32[4,128]{1,0:T(4,128)S(1)}, f32[4,128]{1,0:T(4,128)S(1)}, u32[]{:S(2)}, u32[]{:S(2)}) collective-permute-start(f32[4,128]{1,0:T(4,128)S(1)} %get-tuple-element.9), channel_id=1, source_target_pairs={{0,1},{1,2},{2,3},{4,5},{5,6},{6,7},{8,9},{9,10},{10,11},{12,13},{... | collective-permute-start | bytes 6152 | tf_op jit(solution)/shard_map/ppermute | solution.py:316
  13.1 1.3 %collective-permute-start.1 = (f32[4,128]{1,0:T(4,128)S(1)}, f32[4,128]{1,0:T(4,128)S(1)}, u32[]{:S(2)}, u32[]{:S(2)}) collective-permute-start(f32[4,128]{1,0:T(4,128)S(1)} %get-tuple-element.10), channel_id=1, source_target_pairs={{1,0},{2,1},{3,2},{5,4},{6,5},{7,6},{9,8},{10,9},{11,10},{13,12},{... | collective-permute-start | bytes 6152 | tf_op jit(solution)/shard_map/ppermute | solution.py:319
  14.4 0.1 copy.13.pair_ref
  14.5 0.1 copy.14.wpair_ref
  14.6 3.2 %collective-permute-done.1 = f32[4,128]{1,0:T(4,128)S(1)} collective-permute-done((f32[4,128]{1,0:T(4,128)S(1)}, f32[4,128]{1,0:T(4,128)S(1)}, u32[]{:S(2)}, u32[]{:S(2)}) %collective-permute-start.1) | collective-permute-done | bytes 2080 | tf_op jit(solution)/shard_map/ppermute | solution.py:319
  17.8 1.7 %all-to-all-done = f32[8,6,8,128]{3,2,1,0:T(8,128)S(1)} async-done(((f32[8,6,8,128]{3,2,1,0:T(8,128)}), f32[8,6,8,128]{3,2,1,0:T(8,128)S(1)}, u32[]{:S(2)}, u32[]{:S(2)}) %all-to-all-start) | async-done | bytes 196640 | tf_op jit(solution)/shard_map/all_to_all | solution.py:331
  19.5 43.5 %pair_pass.1 = (f32[24,128]{1,0:T(8,128)}, f32[3,3072]{1,0:T(4,128)}, f32[8,128]{1,0:T(8,128)S(1)}) custom-call(f32[192,128]{1,0:T(8,128)S(1)} %bitcast.28, f32[384,128]{1,0:T(8,128)S(1)} %bitcast.29, f32[32,128]{1,0:T(8,128)S(1)} %bitcast.30, s32[24,14]{1,0:T(8,128)S(1)} %copy.13.pair_ref, s32[24,4]{1,0:T(8,128)S(1)} %copy.14.wpair_ref, s32[1]{0:T(128)} %bitcast.11.place_ref), custom_call_target="tpu_custom_call" | custom-call | tf_op jit(solution)/shard_map/pair_pass/pallas_call | solution.py:279
  63.0 0.7 collective-permute-start.2
  63.7 0.8 %collective-permute-done.2 = f32[8,128]{1,0:T(8,128)S(1)} collective-permute-done((f32[8,128]{1,0:T(8,128)S(1)}, f32[8,128]{1,0:T(8,128)S(1)}, u32[]{:S(2)}, u32[]{:S(2)}) %collective-permute-start.2) | collective-permute-done | bytes 4128 | tf_op jit(solution)/shard_map/ppermute | solution.py:308
  64.5 1.2 %collective-permute-start.3 = (f32[8,128]{1,0:T(8,128)S(1)}, f32[8,128]{1,0:T(8,128)S(1)}, u32[]{:S(2)}, u32[]{:S(2)}) collective-permute-start(f32[8,128]{1,0:T(8,128)S(1)} %max.26), channel_id=1, source_target_pairs={{0,2},{1,3},{2,0},{3,1},{4,6},{5,7},{6,4},{7,5},{8,10},{9,11},{10,... | collective-permute-start | bytes 12296 | tf_op jit(solution)/shard_map/ppermute | solution.py:308
  65.7 2.4 %collective-permute-done.3 = f32[8,128]{1,0:T(8,128)S(1)} collective-permute-done((f32[8,128]{1,0:T(8,128)S(1)}, f32[8,128]{1,0:T(8,128)S(1)}, u32[]{:S(2)}, u32[]{:S(2)}) %collective-permute-start.3) | collective-permute-done | bytes 4128 | tf_op jit(solution)/shard_map/ppermute | solution.py:308
  68.1 2.0 %collective-permute-start.4 = (f32[8,128]{1,0:T(8,128)S(1)}, f32[8,128]{1,0:T(8,128)S(1)}, u32[]{:S(2)}, u32[]{:S(2)}) collective-permute-start(f32[8,128]{1,0:T(8,128)S(1)} %max.27), channel_id=1, source_target_pairs={{0,4},{4,0},{8,12},{12,8},{16,20},{20,16},{24,28},{28,24},{1,5},{5... | collective-permute-start | bytes 12296 | tf_op jit(solution)/shard_map/ppermute | solution.py:308
  70.1 1.6 %collective-permute-done.4 = f32[8,128]{1,0:T(8,128)S(1)} collective-permute-done((f32[8,128]{1,0:T(8,128)S(1)}, f32[8,128]{1,0:T(8,128)S(1)}, u32[]{:S(2)}, u32[]{:S(2)}) %collective-permute-start.4) | collective-permute-done | bytes 4128 | tf_op jit(solution)/shard_map/ppermute | solution.py:308
  71.7 2.0 %collective-permute-start.5 = (f32[8,128]{1,0:T(8,128)S(1)}, f32[8,128]{1,0:T(8,128)S(1)}, u32[]{:S(2)}, u32[]{:S(2)}) collective-permute-start(f32[8,128]{1,0:T(8,128)S(1)} %max.28), channel_id=1, source_target_pairs={{0,8},{4,12},{8,0},{12,4},{16,24},{20,28},{24,16},{28,20},{1,9},{5... | collective-permute-start | bytes 12296 | tf_op jit(solution)/shard_map/ppermute | solution.py:308
  73.7 1.6 %collective-permute-done.5 = f32[8,128]{1,0:T(8,128)S(1)} collective-permute-done((f32[8,128]{1,0:T(8,128)S(1)}, f32[8,128]{1,0:T(8,128)S(1)}, u32[]{:S(2)}, u32[]{:S(2)}) %collective-permute-start.5) | collective-permute-done | bytes 4128 | tf_op jit(solution)/shard_map/ppermute | solution.py:308
  75.3 2.9 %collective-permute-start.6 = (f32[8,128]{1,0:T(8,128)S(1)}, f32[8,128]{1,0:T(8,128)S(1)}, u32[]{:S(2)}, u32[]{:S(2)}) collective-permute-start(f32[8,128]{1,0:T(8,128)S(1)} %max.29), channel_id=1, source_target_pairs={{0,16},{4,20},{8,24},{12,28},{16,0},{20,4},{24,8},{28,12},{1,17},{... | collective-permute-start | bytes 12296 | tf_op jit(solution)/shard_map/ppermute | solution.py:308
  78.2 1.6 %collective-permute-done.6 = f32[8,128]{1,0:T(8,128)S(1)} collective-permute-done((f32[8,128]{1,0:T(8,128)S(1)}, f32[8,128]{1,0:T(8,128)S(1)}, u32[]{:S(2)}, u32[]{:S(2)}) %collective-permute-start.6) | collective-permute-done | bytes 4128 | tf_op jit(solution)/shard_map/ppermute | solution.py:308
  79.8 0.5 slice.19
  (24 shorter events, 0.1 us)
Async XLA Ops:
  0.6 0.7 copy-start
  4.1 7.4 %copy-start.5 = (s32[6]{0:T(128)S(1)}, s32[6]{0:T(128)}, u32[]{:S(2)}) copy-start(s32[6]{0:T(128)} %param.10) | copy-start | bytes 76
  4.1 7.5 %copy-start.2 = (f32[4,768]{1,0:T(4,128)S(1)}, f32[4,768]{1,0:T(4,128)}, u32[]{:S(2)}) copy-start(f32[4,768]{1,0:T(4,128)} %param.9) | copy-start | bytes 36868
  4.1 10.3 %copy-start.3 = (s32[24,14]{0,1:T(8,128)S(1)}, s32[24,14]{0,1:T(8,128)}, u32[]{:S(2)}) copy-start(s32[24,14]{0,1:T(8,128)} %param.8) | copy-start | bytes 4036
  4.1 10.4 %copy-start.4 = (s32[24,4]{0,1:T(4,128)S(1)}, s32[24,4]{0,1:T(4,128)}, u32[]{:S(2)}) copy-start(s32[24,4]{0,1:T(4,128)} %param.11) | copy-start | bytes 1156
  4.1 15.3 %all-to-all-start = ((f32[8,6,8,128]{3,2,1,0:T(8,128)}), f32[8,6,8,128]{3,2,1,0:T(8,128)S(1)}, u32[]{:S(2)}, u32[]{:S(2)}) async-start(f32[8,6,8,128]{3,2,1,0:T(8,128)} %bitcast.6), calls=%async_computation | async-start | bytes 393216 | tf_op jit(solution)/shard_map/all_to_all | solution.py:331
  11.5 8.0 %copy-start.1 = (f32[8,3072]{1,0:T(8,128)S(1)}, f32[8,3072]{1,0:T(8,128)}, u32[]{:S(2)}) copy-start(f32[8,3072]{1,0:T(8,128)} %param.6) | copy-start | bytes 294916
  11.7 3.0 %collective-permute-start = (f32[4,128]{1,0:T(4,128)S(1)}, f32[4,128]{1,0:T(4,128)S(1)}, u32[]{:S(2)}, u32[]{:S(2)}) collective-permute-start(f32[4,128]{1,0:T(4,128)S(1)} %get-tuple-element.9), channel_id=1, source_target_pairs={{0,1},{1,2},{2,3},{4,5},{5,6},{6,7},{8,9},{9,10},{10,11},{12,13},{... | collective-permute-start | bytes 6152 | tf_op jit(solution)/shard_map/ppermute | solution.py:316
  13.1 4.6 %collective-permute-start.1 = (f32[4,128]{1,0:T(4,128)S(1)}, f32[4,128]{1,0:T(4,128)S(1)}, u32[]{:S(2)}, u32[]{:S(2)}) collective-permute-start(f32[4,128]{1,0:T(4,128)S(1)} %get-tuple-element.10), channel_id=1, source_target_pairs={{1,0},{2,1},{3,2},{5,4},{6,5},{7,6},{9,8},{10,9},{11,10},{13,12},{... | collective-permute-start | bytes 6152 | tf_op jit(solution)/shard_map/ppermute | solution.py:319
  63.0 1.5 %collective-permute-start.2 = (f32[8,128]{1,0:T(8,128)S(1)}, f32[8,128]{1,0:T(8,128)S(1)}, u32[]{:S(2)}, u32[]{:S(2)}) collective-permute-start(f32[8,128]{1,0:T(8,128)S(1)} %get-tuple-element.8), channel_id=1, source_target_pairs={{0,1},{1,0},{2,3},{3,2},{4,5},{5,4},{6,7},{7,6},{8,9},{9,8},{10,11... | collective-permute-start | bytes 12296 | tf_op jit(solution)/shard_map/ppermute | solution.py:308
  64.5 3.6 %collective-permute-start.3 = (f32[8,128]{1,0:T(8,128)S(1)}, f32[8,128]{1,0:T(8,128)S(1)}, u32[]{:S(2)}, u32[]{:S(2)}) collective-permute-start(f32[8,128]{1,0:T(8,128)S(1)} %max.26), channel_id=1, source_target_pairs={{0,2},{1,3},{2,0},{3,1},{4,6},{5,7},{6,4},{7,5},{8,10},{9,11},{10,... | collective-permute-start | bytes 12296 | tf_op jit(solution)/shard_map/ppermute | solution.py:308
  68.1 3.6 %collective-permute-start.4 = (f32[8,128]{1,0:T(8,128)S(1)}, f32[8,128]{1,0:T(8,128)S(1)}, u32[]{:S(2)}, u32[]{:S(2)}) collective-permute-start(f32[8,128]{1,0:T(8,128)S(1)} %max.27), channel_id=1, source_target_pairs={{0,4},{4,0},{8,12},{12,8},{16,20},{20,16},{24,28},{28,24},{1,5},{5... | collective-permute-start | bytes 12296 | tf_op jit(solution)/shard_map/ppermute | solution.py:308
  71.7 3.6 %collective-permute-start.5 = (f32[8,128]{1,0:T(8,128)S(1)}, f32[8,128]{1,0:T(8,128)S(1)}, u32[]{:S(2)}, u32[]{:S(2)}) collective-permute-start(f32[8,128]{1,0:T(8,128)S(1)} %max.28), channel_id=1, source_target_pairs={{0,8},{4,12},{8,0},{12,4},{16,24},{20,28},{24,16},{28,20},{1,9},{5... | collective-permute-start | bytes 12296 | tf_op jit(solution)/shard_map/ppermute | solution.py:308
  75.3 4.5 %collective-permute-start.6 = (f32[8,128]{1,0:T(8,128)S(1)}, f32[8,128]{1,0:T(8,128)S(1)}, u32[]{:S(2)}, u32[]{:S(2)}) collective-permute-start(f32[8,128]{1,0:T(8,128)S(1)} %max.29), channel_id=1, source_target_pairs={{0,16},{4,20},{8,24},{12,28},{16,0},{20,4},{24,8},{28,12},{1,17},{... | collective-permute-start | bytes 12296 | tf_op jit(solution)/shard_map/ppermute | solution.py:308
